TPU v7x, 128 devices: a whole 4x4x4 slice. The times are simulated.
128 devices in a mesh: dp: 2 (over core), expert: 64 (over y, x, z).
Axes of the slice: x: 4, y: 4, z: 4, core: 2. Of those that a mesh axis runs over, the one named last changes fastest.
Arguments:
- queries: bfloat16 [32768, 1280], P(('dp', 'expert')), may hold values from -28 to 28
- keys_in: bfloat16 [32768, 1280], P(('dp', 'expert')), may hold values from -16 to 16
- values_in: bfloat16 [32768, 1280], P(('dp', 'expert')), may hold values from -6 to 6
- resid: bfloat16 [32768, 1280], P(('dp', 'expert')), may hold values from -6 to 6
- out_proj: bfloat16 [1280, 1280], replicated, may hold values from -0.15625 to 0.15625
- ln_gain: float32 [1280], replicated, may hold values from 0.25 to 1.75
- w_in: bfloat16 [64, 1280, 2560], P('expert', None, 'dp'), may hold values from -0.15625 to 0.15625
- w_out: bfloat16 [64, 2560, 1280], P('expert', 'dp'), may hold values from -0.125 to 0.125
- route: int32 [4, 32768], P(None, ('dp', 'expert')), may hold values from 0 to 15, as said below
- slot: int32 [4, 32768], P(None, ('dp', 'expert')), may hold values from 0 to 8, as said below
- gates: float32 [4, 32768], P(None, ('dp', 'expert')), may hold values from 0.3 to 1
- cotangent: bfloat16 [4, 32768, 1280], P(None, ('dp', 'expert')), may hold values from -24 to 24
Outputs:
- resid_grad: bfloat16 [32768, 1280], P(('dp', 'expert'))
- query_grad: bfloat16 [32768, 1280], P(('dp', 'expert'))
- key_grad: bfloat16 [32768, 1280], P(('dp', 'expert'))
- value_grad: bfloat16 [32768, 1280], P(('dp', 'expert'))
- proj_grad: float32 [1280, 1280], P(None, ('dp', 'expert'))
- gain_grad: float32 [1280], P(('dp', 'expert'))
- gate_grad: float32 [4, 32768], P(None, ('dp', 'expert'))
- w_in_grad: bfloat16 [64, 1280, 2560], P('expert', None, 'dp')
- w_out_grad: bfloat16 [64, 2560, 1280], P('expert', 'dp')
Inputs may be any that keep to these rules, and one draw needn't show every extreme that they name: route[m, t] names one of the 16 experts of member m. slot[m, t] == 8 marks a dropped token; among the tokens of one device that member m sends to one expert, the kept ones have distinct slots.
All inputs are finite; a program needn't handle non-finite values.
Results may differ from a plain program's by a relative error of at most 0.025.
Values may be sent and summed in bfloat16 or wider, within the bound.
A program may use at most 128 MiB of HBM per device.

v0:
```python
import math

import jax
import jax.numpy as jnp
from jax import lax
from jax.sharding import PartitionSpec as P

HEADS = 16
HEAD = 80
SEQ = 256
CAP = 8


epsilon = 1e-06


def gelu_exact(values):
    return jax.nn.gelu(values, approximate=False)


def attend(query_rows, key_rows, value_rows):
    images = query_rows.shape[0] // SEQ
    shaped = (images, SEQ, HEADS, HEAD)
    query_heads = query_rows.astype(jnp.float32).reshape(shaped)
    key_heads = key_rows.astype(jnp.float32).reshape(shaped)
    value_heads = value_rows.astype(jnp.float32).reshape(shaped)
    scores = jnp.einsum("bqhd,bkhd->bhqk", query_heads, key_heads) / math.sqrt(HEAD)
    weights = jax.nn.softmax(scores, axis=-1).astype(jnp.bfloat16).astype(jnp.float32)
    mixed_heads = jnp.einsum("bhqk,bkhd->bqhd", weights, value_heads)
    return mixed_heads.reshape(query_rows.shape).astype(jnp.bfloat16)


def normed(stream_f, gain):
    average = jnp.mean(stream_f, axis=-1, keepdims=True)
    centred = stream_f - average
    spread_sq = jnp.mean(centred * centred, axis=-1, keepdims=True)
    return centred * lax.rsqrt(spread_sq + epsilon) * gain


def placement(route, slot, n_exp):
    per_member = n_exp // route.shape[0]
    expert_ids = route + per_member * jnp.arange(route.shape[0], dtype=jnp.int32)[:, None]
    kept_mask = slot < CAP
    flat_index = jnp.where(kept_mask, expert_ids * CAP + slot, n_exp * CAP)
    return (kept_mask, flat_index)


def spread_rows(member_rows, flat_index, n_exp):
    width = member_rows.shape[-1]
    buffer = jnp.zeros((n_exp * CAP, width), member_rows.dtype)
    return buffer.at[flat_index.reshape(-1)].set(member_rows.reshape(-1, width), mode="drop")


def pick(buffer, flat_index, kept_mask):
    row_limit = buffer.shape[0] - 1
    picked_rows = buffer[jnp.minimum(flat_index, row_limit)].astype(jnp.float32)
    return jnp.where(kept_mask[..., None], picked_rows, 0.0)


def to_expert(buffer):
    arrived = lax.all_to_all(buffer, "expert", split_axis=0, concat_axis=0, tiled=True)
    return lax.all_gather(arrived, "dp", axis=0, tiled=True)


def to_tokens(partial_sums):
    mine = lax.psum_scatter(
        partial_sums.astype(jnp.bfloat16), "dp", scatter_dimension=0, tiled=True
    )
    return lax.all_to_all(mine, "expert", split_axis=0, concat_axis=0, tiled=True)


def shards(
    queries,
    keys_in,
    values_in,
    resid,
    out_proj,
    ln_gain,
    w_in,
    w_out,
    route,
    slot,
    gates,
    cotangent,
):
    n_exp = lax.axis_size("expert")
    mixed_heads = attend(queries, keys_in, values_in)
    stream = (
        resid.astype(jnp.float32)
        + jnp.dot(mixed_heads, out_proj, preferred_element_type=jnp.float32)
    ).astype(jnp.bfloat16)
    normed_f, norm_back = jax.vjp(normed, stream.astype(jnp.float32), ln_gain)
    entering = normed_f.astype(jnp.bfloat16)
    kept_mask, flat_index = placement(route, slot, n_exp)
    members = route.shape[0]
    tiled_rows = jnp.broadcast_to(entering[None], (members,) + entering.shape)
    expert_rows = to_expert(spread_rows(tiled_rows, flat_index, n_exp))
    w_first = w_in[0]
    w_second = w_out[0]
    pre_act = jnp.dot(expert_rows, w_first, preferred_element_type=jnp.float32)
    hidden = gelu_exact(pre_act).astype(jnp.bfloat16)
    expert_out = to_tokens(jnp.dot(hidden, w_second, preferred_element_type=jnp.float32))
    outputs = pick(expert_out, flat_index, kept_mask)
    cot_f = cotangent.astype(jnp.float32)
    gate_grad = jnp.sum(cot_f * outputs, axis=-1)
    scaled = (gates[..., None] * cot_f).astype(jnp.bfloat16)
    grad_rows = to_expert(spread_rows(scaled, flat_index, n_exp))
    d_hidden = jnp.dot(grad_rows, w_second.T, preferred_element_type=jnp.float32)
    _, gelu_back = jax.vjp(gelu_exact, pre_act)
    d_pre = gelu_back(d_hidden)[0].astype(jnp.bfloat16)
    w_out_grad = jnp.dot(hidden.T, grad_rows, preferred_element_type=jnp.float32).astype(
        jnp.bfloat16
    )[None]
    w_in_grad = jnp.dot(expert_rows.T, d_pre, preferred_element_type=jnp.float32).astype(
        jnp.bfloat16
    )[None]
    back_rows = to_tokens(jnp.dot(d_pre, w_first.T, preferred_element_type=jnp.float32))
    d_norm = jnp.sum(pick(back_rows, flat_index, kept_mask), axis=0)
    d_stream, gain_local = norm_back(d_norm)
    resid_grad = (jnp.sum(cot_f, axis=0) + d_stream).astype(jnp.bfloat16)
    proj_term = jnp.dot(mixed_heads.T, resid_grad, preferred_element_type=jnp.float32)
    proj_grad, gain_grad = (
        lax.psum_scatter(proj_term, ("dp", "expert"), scatter_dimension=1, tiled=True),
        lax.psum_scatter(gain_local, ("dp", "expert"), scatter_dimension=0, tiled=True),
    )
    d_mixed = jnp.dot(resid_grad, out_proj.T, preferred_element_type=jnp.float32).astype(
        jnp.bfloat16
    )
    _, attend_back = jax.vjp(attend, queries, keys_in, values_in)
    query_grad, key_grad, value_grad = attend_back(d_mixed)
    return (
        resid_grad,
        query_grad,
        key_grad,
        value_grad,
        proj_grad,
        gain_grad,
        gate_grad,
        w_in_grad,
        w_out_grad,
    )


def solution(mesh):
    return jax.shard_map(
        shards,
        mesh=mesh,
        in_specs=(
            P(("dp", "expert"), None),
            P(("dp", "expert"), None),
            P(("dp", "expert"), None),
            P(("dp", "expert"), None),
            P(),
            P(),
            P("expert", None, "dp"),
            P("expert", "dp", None),
            P(None, ("dp", "expert")),
            P(None, ("dp", "expert")),
            P(None, ("dp", "expert")),
            P(None, ("dp", "expert"), None),
        ),
        out_specs=(
            P(("dp", "expert"), None),
            P(("dp", "expert"), None),
            P(("dp", "expert"), None),
            P(("dp", "expert"), None),
            P(None, ("dp", "expert")),
            P(("dp", "expert")),
            P(None, ("dp", "expert")),
            P("expert", None, "dp"),
            P("expert", "dp", None),
        ),
        check_vma=False,
    )
```

profile of v0, /device:TPU:0, one launch (start us, length us, event | category | flops | bytes accessed | tf_op | source)
XLA Modules:
  0.0 397.7 jit_solution(8294910582722290537)
XLA Ops:
  8.2 2.2 copy.46
  14.7 4.8 %fusion.45 = (f32[16,256]{1,0:T(8,128)S(1)}, f32[16,256,256]{1,2,0:T(8,128)}) fusion(bf16[256,16,80]{0,2,1:T(8,128)(2,1)} %bitcast.118, bf16[256,16,80]{0,2,1:T(8,128)(2,1)} %bitcast.120), kind=kOutput, calls=%fused_computation.91 | convolution fusion | flops 170918144 | bytes 5521408 | tf_op jit(solution)/shard_map/sub | solution.py:28
  19.5 2.7 divide_convert_fusion
  22.7 2.4 copy-done.18
  29.3 7.2 %scatter_custom_fusion = bf16[512,1280]{1,0:T(8,128)(2,1)} fusion(s32[1024]{0:T(1024)S(1)} %bitcast.126, bf16[1024,1280]{1,0:T(8,128)(2,1)} %bitcast.113, bf16[]{:T(256)} %constant.44.clone.1), kind=kCustom, calls=%fused_computation.71 | custom fusion | bytes 1311232 | tf_op jit(solution)/shard_map/scatter | solution.py:51
  36.4 33.0 %all_to_all.48 = bf16[64,8,1280]{2,1,0:T(8,128)(2,1)} all-to-all(bf16[64,8,1280]{2,1,0:T(8,128)(2,1)} %bitcast.110), channel_id=1, replica_groups=mesh['dp'=2,'expert'=64] {'expert'}, dimensions={0} | all-to-all | bytes 2621440 | tf_op jit(solution)/shard_map/all_to_all | solution.py:61
  69.5 11.7 %all-gather.5.cloned.1.call-start = ((), (), s32[]{:S(2)}) async-start(), calls=%async_computation.7 | async-start | bytes 3932160 | tf_op jit(solution)/shard_map/all_gather | solution.py:62
  81.3 3.7 fusion.3
  85.0 7.2 %scatter_custom_fusion.1 = bf16[512,1280]{1,0:T(8,128)(2,1)} fusion(s32[1024]{0:T(1024)S(1)} %bitcast.127, bf16[1024,1280]{1,0:T(8,128)(2,1)} %bitcast.114, bf16[]{:T(256)} %constant.44.clone.1), kind=kCustom, calls=%fused_computation.69 | custom fusion | bytes 1311232 | tf_op jit(solution)/shard_map/scatter | solution.py:51
  92.2 25.4 %all_to_all.49 = bf16[64,8,1280]{2,1,0:T(8,128)(2,1)} all-to-all(bf16[64,8,1280]{2,1,0:T(8,128)(2,1)} %bitcast.109), channel_id=1, replica_groups=mesh['dp'=2,'expert'=64] {'expert'}, dimensions={0} | all-to-all | bytes 2621440 | tf_op jit(solution)/shard_map/all_to_all | solution.py:61
  117.6 17.2 %multiply_convert_fusion = (bf16[1024,1280]{1,0:T(8,128)(2,1)}, f32[1024,1280]{1,0:T(8,128)}, f32[1024,1280]{1,0:T(8,128)}) fusion(bf16[1024,1280]{1,0:T(8,128)(2,1)} %all-gather.3.cloned.1.call-done, bf16[1,1280,1280]{2,1,0:T(8,128)(2,1)S(1)} %copy-done), kind=kOutput, calls=%fused_computation.21 | convolution fusion | flops 3440640000 | bytes 19005440 | tf_op jit(solution)/shard_map/dot_general | solution.py:100
  134.9 10.3 %add_convert_fusion = bf16[1024,1280]{1,0:T(8,128)(2,1)S(1)} fusion(f32[1024,1280]{1,0:T(8,128)} %get-tuple-element.44, f32[1024,1280]{1,0:T(8,128)} %get-tuple-element.51, bf16[1024,1280]{1,0:T(8,128)(2,1)} %all-gather.5.cloned.1.call-done, bf16[1,1280,1280]{2,1,0:T(8,128)(2,1)} %param.19), kind=kOutput, calls=%fused_computation.22 | convolution fusion | flops 3373793280 | bytes 19005440 | tf_op jit(solution)/shard_map/dot_general | solution.py:108
  146.7 4.9 %convolution_convert_fusion.3 = bf16[1024,1280]{1,0:T(8,128)(2,1)} fusion(bf16[1024,1280]{1,0:T(8,128)(2,1)S(1)} %add_convert_fusion, bf16[1,1280,1280]{2,1,0:T(8,128)(2,1)S(1)} %copy-done), kind=kOutput, calls=%fused_computation.44 | convolution fusion | flops 3356753920 | bytes 8519680 | tf_op jit(solution)/shard_map/dot_general | solution.py:117
  151.7 7.8 %convolution_convert_fusion.2 = bf16[1024,1280]{1,0:T(8,128)(2,1)} fusion(bf16[1024,1280]{1,0:T(8,128)(2,1)} %get-tuple-element.43, bf16[1,1280,1280]{2,1,0:T(8,128)(2,1)} %param.19), kind=kOutput, calls=%fused_computation.43 | convolution fusion | flops 3356753920 | bytes 8519680 | tf_op jit(solution)/shard_map/dot_general | solution.py:102
  160.3 10.7 %all-to-all-start.2 = ((bf16[64,8,1280]{2,1,0:T(8,128)(2,1)}), bf16[64,8,1280]{2,1,0:T(8,128)(2,1)S(1)}, u32[]{:S(2)}, u32[]{:S(2)}) async-start(bf16[64,8,1280]{2,1,0:T(8,128)(2,1)} %bitcast.117), calls=%async_computation.3 | async-start | bytes 2621440 | tf_op jit(solution)/shard_map/all_to_all | solution.py:69
  171.0 6.5 %reduce-scatter.5.cloned.1.call-done = bf16[512,1280]{1,0:T(8,128)(2,1)} async-done(((bf16[1024,1280]{1,0:T(8,128)(2,1)}), bf16[512,1280]{1,0:T(8,128)(2,1)}) %reduce-scatter.5.cloned.1.call-update) | async-done | bytes 1310736 | tf_op jit(solution)/shard_map/reduce_scatter | solution.py:66
  177.5 15.4 %all-to-all-done.2 = bf16[64,8,1280]{2,1,0:T(8,128)(2,1)S(1)} async-done(((bf16[64,8,1280]{2,1,0:T(8,128)(2,1)}), bf16[64,8,1280]{2,1,0:T(8,128)(2,1)S(1)}, u32[]{:S(2)}, u32[]{:S(2)}) %all-to-all-start.2) | async-done | bytes 1310752 | tf_op jit(solution)/shard_map/all_to_all | solution.py:69
  192.9 4.9 %all-to-all-start.3 = ((bf16[64,8,1280]{2,1,0:T(8,128)(2,1)}), bf16[64,8,1280]{2,1,0:T(8,128)(2,1)S(1)}, u32[]{:S(2)}, u32[]{:S(2)}) async-start(bf16[64,8,1280]{2,1,0:T(8,128)(2,1)} %bitcast.116), calls=%async_computation.5 | async-start | bytes 2621440 | tf_op jit(solution)/shard_map/all_to_all | solution.py:69
  197.9 7.9 %fusion.2 = bf16[1,1280,1280]{2,1,0:T(8,128)(2,1)} fusion(bf16[1024,1280]{1,0:T(8,128)(2,1)} %get-tuple-element.43, bf16[1024,1280]{1,0:T(8,128)(2,1)} %all-gather.5.cloned.1.call-done), kind=kOutput, calls=%fused_computation.12 | convolution fusion | flops 3357081600 | bytes 8519680 | tf_op jit(solution)/shard_map/dot_general | solution.py:111
  205.8 5.5 %gather_fusion = bf16[1024,1280]{1,0:T(8,128)(2,1)} fusion(bf16[512,1280]{1,0:T(8,128)(2,1)S(1)} %bitcast.99, s32[1024]{0:T(1024)S(1)} %broadcast_clamp_fusion), kind=kCustom, calls=%fused_computation | custom fusion | bytes 5246976 | tf_op jit(solution)/shard_map/gather | solution.py:56
  211.3 7.1 %all-to-all-done.3 = bf16[64,8,1280]{2,1,0:T(8,128)(2,1)S(1)} async-done(((bf16[64,8,1280]{2,1,0:T(8,128)(2,1)}), bf16[64,8,1280]{2,1,0:T(8,128)(2,1)S(1)}, u32[]{:S(2)}, u32[]{:S(2)}) %all-to-all-start.3) | async-done | bytes 1310752 | tf_op jit(solution)/shard_map/all_to_all | solution.py:69
  218.4 5.5 %gather_fusion.1 = bf16[1024,1280]{1,0:T(8,128)(2,1)} fusion(bf16[512,1280]{1,0:T(8,128)(2,1)S(1)} %bitcast.100, s32[1024]{0:T(1024)S(1)} %broadcast_clamp_fusion), kind=kCustom, calls=%fused_computation.1 | custom fusion | bytes 5246976 | tf_op jit(solution)/shard_map/gather | solution.py:56
  223.8 5.3 %fusion.4 = (f32[4,256]{1,0:T(4,128)}, f32[256,1280]{1,0:T(8,128)S(1)}, f32[256,1280]{1,0:T(8,128)S(1)}) fusion(bf16[4,256,1280]{2,1,0:T(8,128)(2,1)} %param.23, bf16[4,256,1280]{2,1,0:T(8,128)(2,1)} %bitcast.102, pred[4,256]{1,0:T(4,128)(4,1)S(1)} %broadcast_compare_fusion, bf16[4,256,1280]{2,1,0:T(8,128)(2,1)} %bitcast.101), kind=kLoop, calls=%fused_computation.16 | loop fusion | flops 11140096 | bytes 10490880 | tf_op jit(solution)/shard_map/reduce_sum | solution.py:105
  230.6 3.8 fusion.47
  234.4 8.0 %fusion.1 = bf16[1,1280,1280]{2,1,0:T(8,128)(2,1)} fusion(bf16[1024,1280]{1,0:T(8,128)(2,1)} %all-gather.3.cloned.1.call-done, bf16[1024,1280]{1,0:T(8,128)(2,1)} %copy-done.21), kind=kOutput, calls=%fused_computation.11 | convolution fusion | flops 3357081600 | bytes 8519680 | tf_op jit(solution)/shard_map/dot_general | solution.py:114
  244.4 2.3 copy.50
  246.6 2.7 convolution_convert_fusion.7
  251.5 3.6 fusion.16
  257.7 5.1 %convolution_convert_fusion.8 = bf16[16,256,80]{1,2,0:T(8,128)(2,1)} fusion(bf16[256,16,80]{0,2,1:T(8,128)(2,1)} %bitcast.119, f32[16,256,256]{1,2,0:T(8,128)} %get-tuple-element.48, bf16[16,256,256]{1,2,0:T(8,128)(2,1)} %copy-done.13, f32[16,256]{1,0:T(8,128)S(1)} %neg.24, f32[16,256]{1,0:T(8,128)S(1)} %get-tuple-element.47), kind=kOutput, calls=%fused_computation.62 | convolution fusion | flops 173342720 | bytes 7634944 | tf_op jit(solution)/shard_map/transpose(jvp(bqhd,bkhd->bhqk))/dot_general | solution.py:27
  262.7 2.2 copy.55
  264.9 63.0 %all-reduce.1 = f32[1280]{0:T(1024)S(1)} all-reduce(f32[1280]{0:T(1024)S(1)} %get-tuple-element.36), channel_id=4, replica_groups=mesh['dp'=2,'expert'=64] {'dp','expert'}, use_global_device_ids=true, to_apply=%region_14.15.clone | all-reduce | flops 1280 | bytes 10240
  328.5 60.7 %all-reduce.4.cloned.1.call-done = f32[1280,1280]{0,1:T(8,128)} async-done(((f32[1280,1280]{0,1:T(8,128)}), f32[1280,1280]{0,1:T(8,128)}) %all-reduce.4.cloned.1.call-update) | async-done | bytes 6553616
  (84 shorter events, 22.8 us)
Async XLA Ops:
  7.2 110.5 %copy-start = (bf16[1,1280,1280]{2,1,0:T(8,128)(2,1)S(1)}, bf16[1,1280,1280]{2,1,0:T(8,128)(2,1)}, u32[]{:S(2)}) copy-start(bf16[1,1280,1280]{2,1,0:T(8,128)(2,1)} %param.18) | copy-start | bytes 9830404
  7.2 110.4 %all-gather.3.cloned.1.call-start = ((), (), s32[]{:S(2)}) async-start(), calls=%async_computation.6 | async-start | bytes 3932160 | tf_op jit(solution)/shard_map/all_gather | solution.py:62
  19.5 2.7 copy-start.7
  19.5 3.3 copy-start.20
  22.2 4.1 %copy-start.4 = (bf16[16,256,256]{1,2,0:T(8,128)(2,1)}, bf16[16,256,256]{1,2,0:T(8,128)(2,1)S(1)}, u32[]{:S(2)}) copy-start(bf16[16,256,256]{1,2,0:T(8,128)(2,1)S(1)} %divide_convert_fusion) | copy-start | bytes 6291460
  22.2 2.9 copy-start.18
  22.7 3.8 copy-start.9
  25.1 2.2 copy-start.15
  26.3 1.1 copy-start.2
  29.3 52.0 %copy-start.17 = (f32[4,256]{1,0:T(4,128)S(1)}, f32[4,256]{1,0:T(4,128)}, u32[]{:S(2)}) copy-start(f32[4,256]{1,0:T(4,128)} %param.22) | copy-start | bytes 12292
  69.5 65.4 %all-gather.5.cloned.1.call-start = ((), (), s32[]{:S(2)}) async-start(), calls=%async_computation.7 | async-start | bytes 3932160 | tf_op jit(solution)/shard_map/all_gather | solution.py:62
  117.6 42.7 %reduce-scatter.3.cloned.1.call-start = ((), (), s32[]{:S(2)}) async-start(), calls=%async_computation.8 | async-start | bytes 3932160 | tf_op jit(solution)/shard_map/reduce_scatter | solution.py:66
  145.2 1.5 copy-start.21
  151.6 25.9 %reduce-scatter.5.cloned.1.call-start = ((), (), s32[]{:S(2)}) async-start(), calls=%async_computation.9 | async-start | bytes 3932160 | tf_op jit(solution)/shard_map/reduce_scatter | solution.py:66
  159.4 38.4 %copy-start.16 = (s32[4,256]{1,0:T(4,128)S(1)}, s32[4,256]{1,0:T(4,128)}, u32[]{:S(2)}) copy-start(s32[4,256]{1,0:T(4,128)} %param.21) | copy-start | bytes 12292
  160.3 32.6 %all-to-all-start.2 = ((bf16[64,8,1280]{2,1,0:T(8,128)(2,1)}), bf16[64,8,1280]{2,1,0:T(8,128)(2,1)S(1)}, u32[]{:S(2)}, u32[]{:S(2)}) async-start(bf16[64,8,1280]{2,1,0:T(8,128)(2,1)} %bitcast.117), calls=%async_computation.3 | async-start | bytes 2621440 | tf_op jit(solution)/shard_map/all_to_all | solution.py:69
  192.9 25.5 %all-to-all-start.3 = ((bf16[64,8,1280]{2,1,0:T(8,128)(2,1)}), bf16[64,8,1280]{2,1,0:T(8,128)(2,1)S(1)}, u32[]{:S(2)}, u32[]{:S(2)}) async-start(bf16[64,8,1280]{2,1,0:T(8,128)(2,1)} %bitcast.116), calls=%async_computation.5 | async-start | bytes 2621440 | tf_op jit(solution)/shard_map/all_to_all | solution.py:69
  197.8 191.4 %all-reduce.4.cloned.1.call-start = ((), (), s32[]{:S(2)}) async-start(), calls=%async_computation.10 | async-start | bytes 13107200
  223.8 5.3 %copy-start.3 = (f32[256,1280]{1,0:T(8,128)S(1)}, f32[256,1280]{1,0:T(8,128)}, u32[]{:S(2)}) copy-start(f32[256,1280]{1,0:T(8,128)} %copy-done.2) | copy-start | bytes 3932164
  229.5 1.1 copy-start.10
  230.6 3.8 copy-start.11
  234.4 8.0 %copy-start.12 = (bf16[256,1280]{1,0:T(8,128)(2,1)S(1)}, bf16[256,1280]{1,0:T(8,128)(2,1)}, u32[]{:S(2)}) copy-start(bf16[256,1280]{1,0:T(8,128)(2,1)} %copy-done.11) | copy-start | bytes 1966084
  234.4 8.0 %copy-start.19 = (bf16[1280,1280]{1,0:T(8,128)(2,1)S(1)}, bf16[1280,1280]{1,0:T(8,128)(2,1)}, u32[]{:S(2)}) copy-start(bf16[1280,1280]{1,0:T(8,128)(2,1)} %param.16) | copy-start | bytes 9830404
  242.4 4.2 %copy-start.5 = (bf16[16,256,256]{1,2,0:T(8,128)(2,1)S(1)}, bf16[16,256,256]{1,2,0:T(8,128)(2,1)}, u32[]{:S(2)}) copy-start(bf16[16,256,256]{1,2,0:T(8,128)(2,1)} %copy-done.4) | copy-start | bytes 6291460
  244.4 7.1 %copy-start.8 = (bf16[256,1280]{0,1:T(8,128)(2,1)S(1)}, bf16[256,1280]{0,1:T(8,128)(2,1)}, u32[]{:S(2)}) copy-start(bf16[256,1280]{0,1:T(8,128)(2,1)} %copy.48) | copy-start | bytes 1966084
  251.5 3.9 copy-start.6
  251.5 4.0 %copy-start.14 = (bf16[256,1280]{0,1:T(8,128)(2,1)S(1)}, bf16[256,1280]{0,1:T(8,128)(2,1)}, u32[]{:S(2)}) copy-start(bf16[256,1280]{0,1:T(8,128)(2,1)} %copy.47) | copy-start | bytes 1966084
  255.1 1.5 copy-start.13
  257.7 133.1 %copy-start.1 = (bf16[1,1280,1280]{2,1,0:T(8,128)(2,1)S(1)}, bf16[1,1280,1280]{2,1,0:T(8,128)(2,1)}, u32[]{:S(2)}) copy-start(bf16[1,1280,1280]{2,1,0:T(8,128)(2,1)} %param.18) | copy-start | bytes 9830404
Sparse Core Ops, SparseCore 0:
  69.6 9.7 all-gather.2
  117.7 9.7 all-gather.4
  151.7 8.5 reduce-scatter.2
  163.2 14.2 reduce-scatter.4
  234.5 154.5 all-reduce.3
where the time goes:
time: 406 us; the launch traced here: 398 us
  blocking collectives  121 us (30%)
  waiting for transfers between devices  90.5 us (22%)
  matrix products  80.4 us (20%)
  local copies, waits for them, and re-layouts  48.9 us (12%)
  starting transfers between devices  27.5 us (7%)
  between operations  14.6 us (4%)
  other arithmetic  14.4 us (4%)
    unnamed x1, blocking collectives  63 us
    unnamed x6, waiting for transfers between devices  60.8 us
    all_to_all x2, blocking collectives, to_expert(): lax.all_to_all(buffer, 'expert', split_axis=0, concat_axis=0, tiled=True)  58.4 us
    all_to_all x2, waiting for transfers between devices, to_tokens(): lax.all_to_all(mine, 'expert', split_axis=0, concat_axis=0, tiled=True)  22.5 us
    unnamed x54, local copies, waits for them, and re-layouts  19.6 us
    dot_general x1, matrix products, shards(): pre_act = jnp.dot(expert_rows, w_first, preferred_element_type=jnp.float32)  17.2 us
    all_to_all x2, starting transfers between devices, to_tokens(): lax.all_to_all(mine, 'expert', split_axis=0, concat_axis=0, tiled=True)  15.7 us
    scatter x2, local copies, waits for them, and re-layouts, spread_rows(): buffer.at[flat_index.reshape(-1)]  14.4 us
  transfers between devices with their start and end apart: 7, of which 5 were waited for; matrix products, arithmetic and copies ran while one was open for 20% of the time, Pallas kernels for 0%

commit v1 on v0

--- a/solution.py
+++ b/solution.py
@@ -37,24 +37,11 @@
     return centred * lax.rsqrt(spread_sq + epsilon) * gain
 
 
-def placement(route, slot, n_exp):
+def selection(route, slot, n_exp):
     per_member = n_exp // route.shape[0]
-    expert_ids = route + per_member * jnp.arange(route.shape[0], dtype=jnp.int32)[:, None]
-    kept_mask = slot < CAP
-    flat_index = jnp.where(kept_mask, expert_ids * CAP + slot, n_exp * CAP)
-    return (kept_mask, flat_index)
-
-
-def spread_rows(member_rows, flat_index, n_exp):
-    width = member_rows.shape[-1]
-    buffer = jnp.zeros((n_exp * CAP, width), member_rows.dtype)
-    return buffer.at[flat_index.reshape(-1)].set(member_rows.reshape(-1, width), mode="drop")
-
-
-def pick(buffer, flat_index, kept_mask):
-    row_limit = buffer.shape[0] - 1
-    picked_rows = buffer[jnp.minimum(flat_index, row_limit)].astype(jnp.float32)
-    return jnp.where(kept_mask[..., None], picked_rows, 0.0)
+    row = jnp.where(slot < CAP, route * CAP + slot, -1)
+    rows = lax.broadcasted_iota(jnp.int32, (1, per_member * CAP, 1), 1)
+    return rows == row[:, None, :]
 
 
 def to_expert(buffer):
@@ -91,38 +78,47 @@
     ).astype(jnp.bfloat16)
     normed_f, norm_back = jax.vjp(normed, stream.astype(jnp.float32), ln_gain)
     entering = normed_f.astype(jnp.bfloat16)
-    kept_mask, flat_index = placement(route, slot, n_exp)
-    members = route.shape[0]
-    tiled_rows = jnp.broadcast_to(entering[None], (members,) + entering.shape)
-    expert_rows = to_expert(spread_rows(tiled_rows, flat_index, n_exp))
+    one_hot = selection(route, slot, n_exp).astype(jnp.bfloat16)
+    width = entering.shape[-1]
+    cot_f = cotangent.astype(jnp.float32)
+    scaled = (gates[..., None] * cot_f).astype(jnp.bfloat16)
+    grad_rows = jnp.einsum("mrt,mtd->mrd", one_hot, scaled)
+    grad_rows = to_expert(grad_rows.reshape(n_exp, CAP, width)).reshape(-1, width)
+    expert_rows = jnp.einsum("mrt,td->mrd", one_hot, entering)
+    expert_rows = to_expert(expert_rows.reshape(n_exp, CAP, width)).reshape(-1, width)
     w_first = w_in[0]
     w_second = w_out[0]
+    d_hidden = jnp.dot(grad_rows, w_second.T, preferred_element_type=jnp.float32)
     pre_act = jnp.dot(expert_rows, w_first, preferred_element_type=jnp.float32)
-    hidden = gelu_exact(pre_act).astype(jnp.bfloat16)
-    expert_out = to_tokens(jnp.dot(hidden, w_second, preferred_element_type=jnp.float32))
-    outputs = pick(expert_out, flat_index, kept_mask)
-    cot_f = cotangent.astype(jnp.float32)
-    gate_grad = jnp.sum(cot_f * outputs, axis=-1)
-    scaled = (gates[..., None] * cot_f).astype(jnp.bfloat16)
-    grad_rows = to_expert(spread_rows(scaled, flat_index, n_exp))
-    d_hidden = jnp.dot(grad_rows, w_second.T, preferred_element_type=jnp.float32)
-    _, gelu_back = jax.vjp(gelu_exact, pre_act)
+    hidden_f, gelu_back = jax.vjp(gelu_exact, pre_act)
+    hidden = hidden_f.astype(jnp.bfloat16)
+    gate_dot = jnp.sum(hidden.astype(jnp.float32) * d_hidden, axis=-1, keepdims=True)
     d_pre = gelu_back(d_hidden)[0].astype(jnp.bfloat16)
+    back = jnp.dot(d_pre, w_first.T, preferred_element_type=jnp.float32)
+    back = jnp.concatenate([back, jnp.broadcast_to(gate_dot, (back.shape[0], 128))], axis=1)
+    back = to_tokens(back.reshape(-1, CAP, width + 128)).reshape(one_hot.shape[:2] + (width + 128,))
     w_out_grad = jnp.dot(hidden.T, grad_rows, preferred_element_type=jnp.float32).astype(
         jnp.bfloat16
     )[None]
     w_in_grad = jnp.dot(expert_rows.T, d_pre, preferred_element_type=jnp.float32).astype(
         jnp.bfloat16
     )[None]
-    back_rows = to_tokens(jnp.dot(d_pre, w_first.T, preferred_element_type=jnp.float32))
-    d_norm = jnp.sum(pick(back_rows, flat_index, kept_mask), axis=0)
+    gate_rows = back[:, :, width].astype(jnp.float32)
+    gate_grad = jnp.sum(jnp.where(one_hot > 0, gate_rows[:, :, None], 0.0), axis=1) / gates
+    d_norm = jnp.einsum(
+        "mrt,mrd->td", one_hot, back[:, :, :width], preferred_element_type=jnp.float32
+    )
     d_stream, gain_local = norm_back(d_norm)
     resid_grad = (jnp.sum(cot_f, axis=0) + d_stream).astype(jnp.bfloat16)
-    proj_term = jnp.dot(mixed_heads.T, resid_grad, preferred_element_type=jnp.float32)
-    proj_grad, gain_grad = (
-        lax.psum_scatter(proj_term, ("dp", "expert"), scatter_dimension=1, tiled=True),
-        lax.psum_scatter(gain_local, ("dp", "expert"), scatter_dimension=0, tiled=True),
-    )
+    proj_term = jnp.dot(resid_grad.T, mixed_heads, preferred_element_type=jnp.float32)
+    n_dev = 2 * n_exp
+    share = width // n_dev
+    gain_part = jnp.pad(gain_local.reshape(n_dev, 1, share), ((0, 0), (0, 0), (0, width - share)))
+    both = jnp.concatenate([proj_term.reshape(n_dev, share, width), gain_part], axis=1)
+    both = lax.psum_scatter(both.astype(jnp.bfloat16), "dp", scatter_dimension=0, tiled=True)
+    both = lax.all_to_all(both, "expert", split_axis=0, concat_axis=0, tiled=True)
+    both = jnp.sum(both.astype(jnp.float32), axis=0)
+    proj_grad, gain_grad = both[:share].T, both[share, :share]
     d_mixed = jnp.dot(resid_grad, out_proj.T, preferred_element_type=jnp.float32).astype(
         jnp.bfloat16
     )

time: 406 us -> 261 us (0.64); the launches traced: 398 us -> 260 us
  blocking collectives: 121 us -> 57.7 us
  waiting for transfers between devices: 90.5 us -> 53.9 us
  local copies, waits for them, and re-layouts: 48.9 us -> 24.7 us
  starting transfers between devices: 27.5 us -> 16.7 us
  matrix products: 80.4 us -> 73 us
  other arithmetic: 14.4 us -> 19.8 us
    unnamed x1 -> x0, blocking collectives: 63 us -> none
    unnamed x6 -> x4, waiting for transfers between devices: 60.8 us -> 0.07 us
    all_to_all x0 -> x1, waiting for transfers between devices: none -> 18.5 us  [shards(): lax.all_to_all(both, 'expert', split_axis=0, concat_axis=0, tiled=True)]
    scatter x2 -> x0, local copies, waits for them, and re-layouts: 14.4 us -> none  [spread_rows(): buffer.at[flat_index.reshape(-1)]]
    all_gather x2, starting transfers between devices: 11.8 us -> 0.08 us  [to_expert(): return lax.all_gather(arrived, 'dp', axis=0, tiled=True)]
    gather x2 -> x0, local copies, waits for them, and re-layouts: 11 us -> none  [pick(): picked_rows = buffer[jnp.minimum(flat_index, row_limit)].astype(jnp.float32)]
    dot_general x1, matrix products: 17.2 us -> 8.57 us  [shards(): pre_act = jnp.dot(expert_rows, w_first, preferred_element_type=jnp.float32)]
    reduce_scatter x2 -> x1, waiting for transfers between devices: 7.28 us -> 14.6 us  [to_tokens(): lax.psum_scatter(partial_sums.astype(jnp.bfloat16), 'dp', scatter_dimensi...]
  transfers between devices with their start and end apart: 7 -> 6, of which waited for: 5 -> 4; matrix products, arithmetic and copies ran while one was open for 20% -> 21% of each run, Pallas kernels for 0% -> 0%
where the time goes in v1:
time: 261 us; the launch traced here: 260 us
  matrix products  73 us (28%)
  blocking collectives  57.7 us (22%)
  waiting for transfers between devices  53.9 us (21%)
  local copies, waits for them, and re-layouts  24.7 us (9%)
  other arithmetic  19.8 us (8%)
  starting transfers between devices  16.7 us (6%)
  between operations  14.1 us (5%)
    all_to_all x2, blocking collectives, to_expert(): lax.all_to_all(buffer, 'expert', split_axis=0, concat_axis=0, tiled=True)  57.7 us
    all_to_all x1, waiting for transfers between devices, to_tokens(): lax.all_to_all(mine, 'expert', split_axis=0, concat_axis=0, tiled=True)  19.6 us
    all_to_all x1, waiting for transfers between devices, shards(): lax.all_to_all(both, 'expert', split_axis=0, concat_axis=0, tiled=True)  18.5 us
    dot_general x1, matrix products, shards(): jnp.dot(grad_rows, w_second.T, preferred_element_type=jnp.float32)  17.2 us
    unnamed x60, local copies, waits for them, and re-layouts  14.8 us
    reduce_scatter x1, waiting for transfers between devices, to_tokens(): lax.psum_scatter(partial_sums.astype(jnp.bfloat16), 'dp', scatter_dimensi...  14.6 us
    all_to_all x1, starting transfers between devices, to_tokens(): lax.all_to_all(mine, 'expert', split_axis=0, concat_axis=0, tiled=True)  10.6 us
    dot_general x2, matrix products, attend(): jnp.einsum('bqhd,bkhd->bhqk', query_heads, key_heads) / math.sqrt(HEAD)  8.9 us
  transfers between devices with their start and end apart: 6, of which 4 were waited for; matrix products, arithmetic and copies ran while one was open for 21% of the time, Pallas kernels for 0%

profile of v1, /device:TPU:0, one launch (start us, length us, event | category | flops | bytes accessed | tf_op | source)
XLA Modules:
  0.0 260.0 jit_solution(8097112611876001214)
XLA Ops:
  7.2 2.3 copy.55
  9.6 2.2 copy.56
  11.7 2.2 copy.57
  13.9 4.9 %fusion.55 = (f32[16,256]{1,0:T(8,128)S(1)}, f32[16,256,256]{1,2,0:T(8,128)}) fusion(bf16[256,16,80]{0,2,1:T(8,128)(2,1)} %bitcast.107, bf16[256,16,80]{0,2,1:T(8,128)(2,1)} %bitcast.105), kind=kOutput, calls=%fused_computation.98 | convolution fusion | flops 170918144 | bytes 5521408 | tf_op jit(solution)/shard_map/sub | solution.py:28
  18.8 2.8 %divide_convert_fusion = bf16[16,256,256]{1,2,0:T(8,128)(2,1)S(1)} fusion(f32[16,256,256]{1,2,0:T(8,128)} %get-tuple-element.45, f32[16,256]{1,0:T(8,128)S(1)} %get-tuple-element.44), kind=kLoop, calls=%fused_computation.36 | loop fusion | flops 2097152 | bytes 6307840 | tf_op jit(solution)/shard_map/convert_element_type | solution.py:28
  25.4 32.8 %all_to_all.20 = bf16[64,8,1280]{2,1,0:T(8,128)(2,1)} all-to-all(bf16[64,8,1280]{2,1,0:T(8,128)(2,1)S(1)} %bitcast.97), channel_id=1, replica_groups=mesh['dp'=2,'expert'=64] {'expert'}, dimensions={0} | all-to-all | bytes 2621440 | tf_op jit(solution)/shard_map/all_to_all | solution.py:48
  58.3 2.7 %fusion.25 = bf16[4,128,1280]{2,1,0:T(8,128)(2,1)S(1)} fusion(bf16[4,256,1280]{2,1,0:T(8,128)(2,1)} %param.23, f32[4,256]{1,0:T(4,128)S(1)} %copy-done.18, s32[4,256]{1,0:T(4,128)S(1)} %add_select_fusion), kind=kOutput, calls=%fused_computation.51 | convolution fusion | flops 339607552 | bytes 3940352 | tf_op jit(solution)/shard_map/mrt,mtd->mrd/dot_general | solution.py:85
  61.0 24.8 %all_to_all.21 = bf16[64,8,1280]{2,1,0:T(8,128)(2,1)} all-to-all(bf16[64,8,1280]{2,1,0:T(8,128)(2,1)S(1)} %bitcast.98), channel_id=1, replica_groups=mesh['dp'=2,'expert'=64] {'expert'}, dimensions={0} | all-to-all | bytes 2621440 | tf_op jit(solution)/shard_map/all_to_all | solution.py:48
  86.1 8.6 %fusion.21 = f32[1024,1280]{1,0:T(8,128)} fusion(bf16[1,1280,1280]{2,1,0:T(8,128)(2,1)} %param.18, bf16[128,8,1280]{2,1,0:T(8,128)(2,1)} %all-gather.3.cloned.1.call-done), kind=kOutput, calls=%fused_computation.46 | convolution fusion | flops 3355443200 | bytes 11141120 | tf_op jit(solution)/shard_map/dot_general | solution.py:92
  95.8 17.2 %add_convert_fusion = (bf16[1024,1280]{1,0:T(8,128)(2,1)S(1)}, f32[1024,1280]{1,0:T(8,128)S(1)}, f32[1024,1280]{1,0:T(8,128)}) fusion(f32[1024,1280]{1,0:T(8,128)} %fusion.21, bf16[1,1280,1280]{2,1,0:T(8,128)(2,1)S(1)} %copy-done, bf16[128,8,1280]{2,1,0:T(8,128)(2,1)} %all-gather.5.cloned.1.call-done), kind=kOutput, calls=%fused_computation.17 | convolution fusion | flops 3449815040 | bytes 24248320 | tf_op jit(solution)/shard_map/dot_general | solution.py:91
  113.0 3.8 %convolution_convert_fusion.3 = bf16[1024,1280]{1,0:T(8,128)(2,1)S(1)} fusion(bf16[1024,1280]{1,0:T(8,128)(2,1)S(1)} %get-tuple-element.40, bf16[1,1280,1280]{2,1,0:T(8,128)(2,1)S(1)} %copy-done.21), kind=kOutput, calls=%fused_computation.39 | convolution fusion | flops 3356753920 | bytes 8519680 | tf_op jit(solution)/shard_map/dot_general | solution.py:97
  116.8 4.8 %multiply_reduce_fusion = (bf16[1024]{0:T(1024)(128)(2,1)S(1)}, bf16[1024,1280]{1,0:T(8,128)(2,1)}) fusion(f32[1024,1280]{1,0:T(8,128)} %get-tuple-element.48, f32[1024,1280]{1,0:T(8,128)S(1)} %get-tuple-element.41, f32[1024,1280]{1,0:T(8,128)S(1)} %copy-done.8), kind=kLoop, calls=%fused_computation.15 | loop fusion | flops 7863296 | bytes 18352128 | tf_op jit(solution)/shard_map/reduce_sum | solution.py:95
  123.6 14.6 %reduce-scatter.3.cloned.1.call-done = bf16[64,8,1408]{2,1,0:T(8,128)(2,1)} async-done(((bf16[128,8,1408]{2,1,0:T(8,128)(2,1)}), bf16[64,8,1408]{2,1,0:T(8,128)(2,1)}) %reduce-scatter.3.cloned.1.call-update) | async-done | bytes 1441808 | tf_op jit(solution)/shard_map/reduce_scatter | solution.py:53
  138.2 10.6 %all-to-all-start.2 = ((bf16[64,8,1408]{2,1,0:T(8,128)(2,1)}), bf16[64,8,1408]{2,1,0:T(8,128)(2,1)S(1)}, u32[]{:S(2)}, u32[]{:S(2)}) async-start(bf16[64,8,1408]{2,1,0:T(8,128)(2,1)} %reduce-scatter.3.cloned.1.call-done), calls=%async_computation.3 | async-start | bytes 2883584 | tf_op jit(solution)/shard_map/all_to_all | solution.py:56
  149.0 3.3 %convert_reduce_fusion = f32[256,1280]{1,0:T(8,128)} fusion(bf16[4,256,1280]{2,1,0:T(8,128)(2,1)} %param.23), kind=kLoop, calls=%fused_computation.7 | loop fusion | flops 2293760 | bytes 3932160 | tf_op jit(solution)/shard_map/reduce_sum | solution.py:112
  152.3 19.6 %all-to-all-done.2 = bf16[64,8,1408]{2,1,0:T(8,128)(2,1)S(1)} async-done(((bf16[64,8,1408]{2,1,0:T(8,128)(2,1)}), bf16[64,8,1408]{2,1,0:T(8,128)(2,1)S(1)}, u32[]{:S(2)}, u32[]{:S(2)}) %all-to-all-start.2) | async-done | bytes 1441824 | tf_op jit(solution)/shard_map/all_to_all | solution.py:56
  175.6 2.7 %convolution_convert_fusion.2 = bf16[128,10,1280]{2,0,1:T(8,128)(2,1)S(1)} fusion(bf16[256,1280,1]{0,1,2:T(8,128)(2,1)} %bitcast.100, bf16[128,10,256]{2,1,0:T(8,128)(2,1)} %dot_general.71), kind=kOutput, calls=%fused_computation.38 | convolution fusion | flops 840499200 | bytes 4587520 | tf_op jit(solution)/shard_map/dot_general | solution.py:113
  178.2 2.0 fusion.17
  180.3 8.0 %fusion.2 = bf16[1,1280,1280]{2,1,0:T(8,128)(2,1)} fusion(bf16[1024,1280]{1,0:T(8,128)(2,1)} %copy-done.26, bf16[128,8,1280]{2,1,0:T(8,128)(2,1)} %all-gather.3.cloned.1.call-done), kind=kOutput, calls=%fused_computation.8 | convolution fusion | flops 3357081600 | bytes 8519680 | tf_op jit(solution)/shard_map/dot_general | solution.py:103
  188.4 5.3 %fusion.3 = bf16[1,1280,1280]{2,1,0:T(8,128)(2,1)} fusion(bf16[1024,1280]{1,0:T(8,128)(2,1)S(1)} %copy-done.10, bf16[128,8,1280]{2,1,0:T(8,128)(2,1)S(1)} %copy-done.24), kind=kOutput, calls=%fused_computation.9 | convolution fusion | flops 3357081600 | bytes 8519680 | tf_op jit(solution)/shard_map/dot_general | solution.py:100
  195.5 2.2 copy.61
  197.8 2.7 %convolution_convert_fusion.7 = bf16[16,80,256]{2,1,0:T(8,128)(2,1)} fusion(bf16[16,80,256]{2,1,0:T(8,128)(2,1)} %bitcast.95, bf16[16,256,256]{1,2,0:T(8,128)(2,1)S(1)} %copy-done.3), kind=kOutput, calls=%fused_computation.64 | convolution fusion | flops 168099840 | bytes 3407872 | tf_op jit(solution)/shard_map/transpose(jvp(bhqk,bkhd->bqhd))/dot_general | solution.py:29
  200.4 2.2 copy.71
  202.6 3.2 %fusion.15 = (f32[16,256]{1,0:T(8,128)S(1)}, bf16[16,256,256]{1,2,0:T(8,128)(2,1)S(1)}) fusion(f32[16,256,256]{1,2,0:T(8,128)} %get-tuple-element.45, f32[16,256]{1,0:T(8,128)S(1)} %multiply_divide_fusion, bf16[16,80,256]{2,1,0:T(8,128)(2,1)} %bitcast.96, bf16[256,16,80]{0,2,1:T(8,128)(2,1)S(1)} %bitcast.94), kind=kOutput, calls=%fused_computation.35 | convolution fusion | flops 173010944 | bytes 7634944 | tf_op jit(solution)/shard_map/transpose(jvp(bhqk,bkhd->bqhd))/dot_general | solution.py:29
  205.9 4.8 %copy.68 = bf16[64,11,1280]{2,1,0:T(8,128)(2,1)} copy(bf16[64,11,1280]{2,0,1:T(8,128)(2,1)} %reduce-scatter.5.cloned.1.call-done) | data formatting | bytes 3604480 | tf_op jit(solution)/shard_map/reduce_scatter | solution.py:118
  210.7 5.6 %all-to-all-start.3 = ((bf16[64,11,1280]{2,1,0:T(8,128)(2,1)}), bf16[64,11,1280]{2,1,0:T(8,128)(2,1)}, u32[]{:S(2)}, u32[]{:S(2)}) async-start(bf16[64,11,1280]{2,1,0:T(8,128)(2,1)} %copy.68), calls=%async_computation.5 | async-start | bytes 5242880 | tf_op jit(solution)/shard_map/all_to_all | solution.py:119
  216.3 4.0 %convolution_convert_fusion.8 = bf16[16,256,80]{1,2,0:T(8,128)(2,1)} fusion(bf16[256,16,80]{0,2,1:T(8,128)(2,1)S(1)} %bitcast.108, f32[16,256,256]{1,2,0:T(8,128)} %get-tuple-element.45, bf16[16,256,256]{1,2,0:T(8,128)(2,1)S(1)} %get-tuple-element.51, f32[16,256]{1,0:T(8,128)S(1)} %neg.23, f32[16,256]{1,0:T(8,128)S(1)} %get-tuple-element.44), kind=kOutput, calls=%fused_computation.65 | convolution fusion | flops 173342720 | bytes 7634944 | tf_op jit(solution)/shard_map/transpose(jvp(bqhd,bkhd->bhqk))/dot_general | solution.py:27
  220.4 2.2 copy.70
  222.5 4.9 %convolution_convert_fusion.9 = bf16[16,256,80]{1,2,0:T(8,128)(2,1)} fusion(bf16[256,16,80]{0,2,1:T(8,128)(2,1)} %bitcast.106, f32[16,256,256]{1,2,0:T(8,128)} %get-tuple-element.45, bf16[16,256,256]{1,2,0:T(8,128)(2,1)} %copy-done.14, f32[16,256]{1,0:T(8,128)S(1)} %neg.23, f32[16,256]{1,0:T(8,128)S(1)} %get-tuple-element.44), kind=kOutput, calls=%fused_computation.66 | convolution fusion | flops 173342720 | bytes 7634944 | tf_op jit(solution)/shard_map/transpose(jvp(bqhd,bkhd->bhqk))/dot_general | solution.py:27
  227.4 2.2 copy.69
  231.6 18.5 %all-to-all-done.3 = bf16[64,11,1280]{2,1,0:T(8,128)(2,1)} async-done(((bf16[64,11,1280]{2,1,0:T(8,128)(2,1)}), bf16[64,11,1280]{2,1,0:T(8,128)(2,1)}, u32[]{:S(2)}, u32[]{:S(2)}) %all-to-all-start.3) | async-done | bytes 1802272 | tf_op jit(solution)/shard_map/all_to_all | solution.py:119
  250.1 2.2 convert_reduce_fusion.1
  (90 shorter events, 16.2 us)
Async XLA Ops:
  7.2 88.6 %copy-start = (bf16[1,1280,1280]{2,1,0:T(8,128)(2,1)S(1)}, bf16[1,1280,1280]{2,1,0:T(8,128)(2,1)}, u32[]{:S(2)}) copy-start(bf16[1,1280,1280]{2,1,0:T(8,128)(2,1)} %param.19) | copy-start | bytes 9830404
  7.2 78.9 %all-gather.3.cloned.1.call-start = ((), (), s32[]{:S(2)}) async-start(), calls=%async_computation.6 | async-start | bytes 3932160 | tf_op jit(solution)/shard_map/all_gather | solution.py:49
  18.8 2.8 %copy-start.6 = (bf16[256,1280]{0,1:T(8,128)(2,1)S(1)}, bf16[256,1280]{0,1:T(8,128)(2,1)}, u32[]{:S(2)}) copy-start(bf16[256,1280]{0,1:T(8,128)(2,1)} %copy.57) | copy-start | bytes 1966084
  18.8 3.4 %copy-start.22 = (bf16[1280,1280]{1,0:T(8,128)(2,1)S(1)}, bf16[1280,1280]{1,0:T(8,128)(2,1)}, u32[]{:S(2)}) copy-start(bf16[1280,1280]{1,0:T(8,128)(2,1)} %param.16) | copy-start | bytes 9830404
  18.8 3.5 %copy-start.25 = (bf16[256,1280]{1,0:T(8,128)(2,1)S(1)}, bf16[256,1280]{1,0:T(8,128)(2,1)}, u32[]{:S(2)}) copy-start(bf16[256,1280]{1,0:T(8,128)(2,1)} %param.15) | copy-start | bytes 1966084
  21.5 1.9 copy-start.2
  22.1 1.7 copy-start.11
  22.1 1.7 copy-start.19
  22.1 1.7 copy-start.20
  22.1 2.4 copy-start.17
  23.5 34.9 %copy-start.18 = (f32[4,256]{1,0:T(4,128)S(1)}, f32[4,256]{1,0:T(4,128)}, u32[]{:S(2)}) copy-start(f32[4,256]{1,0:T(4,128)} %param.22) | copy-start | bytes 12292
  58.3 37.5 %all-gather.5.cloned.1.call-start = ((), (), s32[]{:S(2)}) async-start(), calls=%async_computation.7 | async-start | bytes 3932160 | tf_op jit(solution)/shard_map/all_gather | solution.py:49
  85.9 52.3 %reduce-scatter.3.cloned.1.call-start = ((), (), s32[]{:S(2)}) async-start(), calls=%async_computation.8 | async-start | bytes 4325376 | tf_op jit(solution)/shard_map/reduce_scatter | solution.py:53
  95.8 17.2 %copy-start.21 = (bf16[1,1280,1280]{2,1,0:T(8,128)(2,1)S(1)}, bf16[1,1280,1280]{2,1,0:T(8,128)(2,1)}, u32[]{:S(2)}) copy-start(bf16[1,1280,1280]{2,1,0:T(8,128)(2,1)} %param.18) | copy-start | bytes 9830404
  113.0 3.8 %copy-start.26 = (bf16[1024,1280]{1,0:T(8,128)(2,1)}, bf16[1024,1280]{1,0:T(8,128)(2,1)S(1)}, u32[]{:S(2)}) copy-start(bf16[1024,1280]{1,0:T(8,128)(2,1)S(1)} %get-tuple-element.40) | copy-start | bytes 7864324
  113.0 3.8 %copy-start.8 = (f32[1024,1280]{1,0:T(8,128)S(1)}, f32[1024,1280]{1,0:T(8,128)}, u32[]{:S(2)}) copy-start(f32[1024,1280]{1,0:T(8,128)} %fusion.21) | copy-start | bytes 15728644
  123.6 48.4 %copy-start.5 = (f32[256,1280]{1,0:T(8,128)S(1)}, f32[256,1280]{1,0:T(8,128)}, u32[]{:S(2)}) copy-start(f32[256,1280]{1,0:T(8,128)} %copy-done.4) | copy-start | bytes 3932164
  138.2 33.7 %all-to-all-start.2 = ((bf16[64,8,1408]{2,1,0:T(8,128)(2,1)}), bf16[64,8,1408]{2,1,0:T(8,128)(2,1)S(1)}, u32[]{:S(2)}, u32[]{:S(2)}) async-start(bf16[64,8,1408]{2,1,0:T(8,128)(2,1)} %reduce-scatter.3.cloned.1.call-done), calls=%async_computation.3 | async-start | bytes 2883584 | tf_op jit(solution)/shard_map/all_to_all | solution.py:56
  148.8 57.2 %reduce-scatter.5.cloned.1.call-start = ((), (), s32[]{:S(2)}) async-start(), calls=%async_computation.9 | async-start | bytes 5406720 | tf_op jit(solution)/shard_map/reduce_scatter | solution.py:118
  171.9 1.1 copy-start.15
  171.9 1.8 copy-start.9
  174.0 1.6 copy-start.12
  180.3 8.0 %copy-start.10 = (bf16[1024,1280]{1,0:T(8,128)(2,1)S(1)}, bf16[1024,1280]{1,0:T(8,128)(2,1)}, u32[]{:S(2)}) copy-start(bf16[1024,1280]{1,0:T(8,128)(2,1)} %get-tuple-element.43) | copy-start | bytes 7864324
  180.3 8.0 %copy-start.24 = (bf16[128,8,1280]{2,1,0:T(8,128)(2,1)S(1)}, bf16[128,8,1280]{2,1,0:T(8,128)(2,1)}, u32[]{:S(2)}) copy-start(bf16[128,8,1280]{2,1,0:T(8,128)(2,1)} %all-gather.5.cloned.1.call-done) | copy-start | bytes 7864324
  188.3 5.3 %copy-start.13 = (bf16[256,1280]{1,0:T(8,128)(2,1)S(1)}, bf16[256,1280]{1,0:T(8,128)(2,1)}, u32[]{:S(2)}) copy-start(bf16[256,1280]{1,0:T(8,128)(2,1)} %copy-done.12) | copy-start | bytes 1966084
  188.3 5.3 %copy-start.23 = (bf16[1280,1280]{1,0:T(8,128)(2,1)S(1)}, bf16[1280,1280]{1,0:T(8,128)(2,1)}, u32[]{:S(2)}) copy-start(bf16[1280,1280]{1,0:T(8,128)(2,1)} %param.16) | copy-start | bytes 9830404
  193.6 4.1 %copy-start.3 = (bf16[16,256,256]{1,2,0:T(8,128)(2,1)S(1)}, bf16[16,256,256]{1,2,0:T(8,128)(2,1)}, u32[]{:S(2)}) copy-start(bf16[16,256,256]{1,2,0:T(8,128)(2,1)} %copy-done.2) | copy-start | bytes 6291460
  195.5 7.1 %copy-start.7 = (bf16[256,1280]{0,1:T(8,128)(2,1)S(1)}, bf16[256,1280]{0,1:T(8,128)(2,1)}, u32[]{:S(2)}) copy-start(bf16[256,1280]{0,1:T(8,128)(2,1)} %copy.57) | copy-start | bytes 1966084
  205.9 10.4 %copy-start.14 = (bf16[16,256,256]{1,2,0:T(8,128)(2,1)}, bf16[16,256,256]{1,2,0:T(8,128)(2,1)S(1)}, u32[]{:S(2)}) copy-start(bf16[16,256,256]{1,2,0:T(8,128)(2,1)S(1)} %get-tuple-element.51) | copy-start | bytes 6291460
  205.9 10.4 %copy-start.16 = (bf16[256,1280]{0,1:T(8,128)(2,1)S(1)}, bf16[256,1280]{0,1:T(8,128)(2,1)}, u32[]{:S(2)}) copy-start(bf16[256,1280]{0,1:T(8,128)(2,1)} %copy.55) | copy-start | bytes 1966084
  210.7 39.3 %all-to-all-start.3 = ((bf16[64,11,1280]{2,1,0:T(8,128)(2,1)}), bf16[64,11,1280]{2,1,0:T(8,128)(2,1)}, u32[]{:S(2)}, u32[]{:S(2)}) async-start(bf16[64,11,1280]{2,1,0:T(8,128)(2,1)} %copy.68), calls=%async_computation.5 | async-start | bytes 5242880 | tf_op jit(solution)/shard_map/all_to_all | solution.py:119
  222.5 30.9 %copy-start.1 = (bf16[1,1280,1280]{2,1,0:T(8,128)(2,1)S(1)}, bf16[1,1280,1280]{2,1,0:T(8,128)(2,1)}, u32[]{:S(2)}) copy-start(bf16[1,1280,1280]{2,1,0:T(8,128)(2,1)} %param.19) | copy-start | bytes 9830404
  (1 other events, 1.1 us)
Sparse Core Ops, SparseCore 0:
  58.4 9.7 all-gather.2
  86.0 9.7 all-gather.4
  123.7 14.4 reduce-scatter.2
  180.4 10.1 reduce-scatter.4

commit v2 on v1

v2 whole, which is shorter than its diff:
```python
import functools
import math

import jax
import jax.numpy as jnp
import numpy as np
from jax import lax
from jax.experimental import pallas as pl
from jax.experimental.pallas import tpu as pltpu
from jax.sharding import PartitionSpec as P

D = 1280
HALF = 640
HEADS = 16
HEAD = 80
TOK = 256
MEMBERS = 4
CAP = 8
CHIPS = 64
ROWS = CHIPS * CAP
BLOCK = 256
H = 2560
LANES = 512
SHARE = 10
EPS = 1e-06
MESH = pl.DeviceIdType.MESH
F32 = jnp.float32
BF16 = jnp.bfloat16


def product(a, b, contract):
    return lax.dot_general(a, b, (((contract[0],), (contract[1],)), ((), ())), preferred_element_type=F32)


def nn(a, b):
    return product(a, b, (1, 0))


def nt(a, b):
    return product(a, b, (1, 1))


def tn(a, b):
    return product(a, b, (0, 0))


def two_lanes(ref, n, *lead):
    low = pl.multiple_of(n * 128, 128)
    high = pl.multiple_of(HALF + n * 128, 128)
    return jnp.concatenate([ref[(*lead, slice(None), pl.ds(low, 128))], ref[(*lead, slice(None), pl.ds(high, 128))]], axis=1)


def pack(rows):
    count = rows.shape[0] // CAP
    low = rows[:, :128].reshape(count, CAP, 128)
    high = rows[:, 128:].reshape(count, CAP, 128)
    return jnp.concatenate([low, high], axis=1).astype(BF16)


def gelu_with_grad(x):
    u = 1.0 / (1.0 + (0.3275911 * math.sqrt(0.5)) * jnp.abs(x))
    poly = u * (0.254829592 + u * (-0.284496736 + u * (1.421413741 + u * (-1.453152027 + u * 1.061405429))))
    e = jnp.exp(-0.5 * x * x)
    tail = 0.5 * poly * e
    cdf = jnp.where(x >= 0.0, 1.0 - tail, tail)
    return x * cdf, cdf + x * (e * (1.0 / math.sqrt(2.0 * math.pi)))


def block_orders():
    d = np.arange(HALF)
    y, x, z, r = d // 160, (d // 40) % 4, (d // 10) % 4, d % 10
    out = np.zeros((2, HALF, HALF), np.float32)
    out[0, d, x * 160 + y * 40 + z * 10 + r] = 1.0
    out[1, d, z * 160 + y * 40 + x * 10 + r] = 1.0
    return out


def kernel(
    q_in, k_in, v_in, res_in, proj_in, gain_ref, first_in, second_in, route_ref, slot_ref, gates_ref, cot_in, order_in,
    resid_out, q_out, k_out, v_out, share_out, gate_out, first_out, second_out,
    q_v, k_v, v_v, res_v, proj_v, cot_v, order_v, first_v, second_v,
    attn_v, acc_v, mixed_v, mixed_p, rstd_v, enter_v, pick_v,
    send_a, send_b, grad_recv, enter_recv, back_recv,
    grad_v, enter_rows, grad_p, enter_p, hidden_v, dpre_v, hidden_p, dpre_p, dot_v,
    rg_v, rg_p, perm_v, resid_v, dmix_v, gate_send, gate_recv,
    sum1, recv1, sum2, recv2, sum3, recv3,
    load_sem, store_sem, local_sem, pair_send, pair_recv, a2a_send, a2a_recv, rs_send, rs_recv,
):
    core = lax.axis_index("dp")
    chip = lax.axis_index("expert")
    place = (chip // 16, (chip // 4) % 4, chip % 4)

    def offsets(n):
        q = n // 16
        return ((q % 2) * 2 + q // 2, (n // 4) % 4, n % 4)

    def ahead(n):
        o = offsets(n)
        return ((place[0] + o[0]) % 4) * 16 + ((place[1] + o[1]) % 4) * 4 + (place[2] + o[2]) % 4

    def behind(n):
        o = offsets(n)
        return ((place[0] + 4 - o[0]) % 4) * 16 + ((place[1] + 4 - o[1]) % 4) * 4 + (place[2] + 4 - o[2]) % 4

    def load(n, src, dst):
        return pltpu.make_async_copy(src, dst, load_sem.at[n])

    loads = [
        load(0, cot_in, cot_v),
        load(1, q_in, q_v),
        load(2, k_in, k_v),
        load(3, v_in, v_v),
        load(4, proj_in, proj_v),
        load(5, res_in, res_v),
        load(6, second_in.at[0], second_v.at[pl.ds(0, D)]),
        load(7, first_in.at[0], first_v.at[:, pl.ds(0, D)]),
        load(8, order_in, order_v),
    ]
    for item in loads:
        item.start()

    barrier = pltpu.get_barrier_semaphore()

    @pl.loop(1, CHIPS)
    def _(n):
        pl.semaphore_signal(barrier, inc=1, device_id=(core, ahead(n)), device_id_type=MESH)

    pl.semaphore_signal(barrier, inc=1, device_id=(1 - core, chip), device_id_type=MESH)

    def pair(n, src, dst):
        return pltpu.make_async_remote_copy(
            src, dst, pair_send.at[n], pair_recv.at[n], device_id=(1 - core, chip), device_id_type=MESH
        )

    row_iota = lax.broadcasted_iota(jnp.int32, (MEMBERS * 32, TOK), 0)
    row_of = jnp.where(slot_ref[...] < CAP, route_ref[...] * CAP + slot_ref[...], -1)
    loads[0].wait()
    for m in range(MEMBERS):
        picked = jnp.where(row_iota == row_of[m : m + 1, :], 1.0, 0.0)
        pick_v[m * 128 : (m + 1) * 128, :] = picked.astype(BF16)
        gate_rows = jnp.sum(picked * gates_ref[m : m + 1, :], axis=1, keepdims=True)

        @pl.loop(0, 5)
        def _(n, m=m, gate_rows=gate_rows):
            rows = nn(pick_v[m * 128 : (m + 1) * 128, :], two_lanes(cot_v, n, m)) * gate_rows
            send_a[m * 16 : (m + 1) * 16, :, pl.ds(pl.multiple_of(n * 128, 128), 128)] = pack(rows)

    pl.semaphore_wait(barrier, CHIPS)

    pair_second = pair(0, second_in.at[0], second_v.at[pl.ds(D, D)])
    pair_first = pair(1, first_in.at[0], first_v.at[:, pl.ds(D, D)])
    pair_second.start()
    pair_first.start()

    def dispatch(which, src, dst):
        own = pltpu.make_async_copy(src.at[chip], dst.at[0], local_sem.at[which])
        own.start()

        @pl.loop(1, CHIPS)
        def _(n):
            to = ahead(n)
            pltpu.make_async_remote_copy(
                src.at[to], dst.at[n], a2a_send.at[which], a2a_recv.at[which * 2 + n // 32],
                device_id=(core, to), device_id_type=MESH,
            ).start()

        return own

    def wait_sent(which, ref, count):
        pltpu.make_async_remote_copy(
            ref.at[pl.ds(0, count)], ref.at[pl.ds(0, count)], a2a_send.at[which], a2a_recv.at[which * 2],
            device_id=(1 - core, chip), device_id_type=MESH,
        ).wait_send()

    def wait_landed(n, ref, start, count):
        pltpu.make_async_remote_copy(
            ref.at[pl.ds(start, count)], ref.at[pl.ds(start, count)], a2a_send.at[0], a2a_recv.at[n],
            device_id=(1 - core, chip), device_id_type=MESH,
        ).wait_recv()

    own_grad = dispatch(0, send_a, grad_recv)

    def head_window(h):
        tile = (h * HEAD) // 128
        tile = tile - tile // 9
        lanes = lax.broadcasted_iota(jnp.int32, (1, 256), 1)
        first = h * HEAD - tile * 128
        inside = jnp.where((lanes >= first) & (lanes < first + HEAD), 1.0, 0.0).astype(BF16)
        return pl.ds(pl.multiple_of(tile * 128, 128), 256), inside

    acc_v[0] = jnp.zeros((TOK, D), F32)
    loads[1].wait()
    loads[2].wait()
    loads[3].wait()
    scale = 1.0 / math.sqrt(HEAD)

    @pl.loop(0, HEADS // 2)
    def _(pair_of):
        for one in range(2):
            h = pair_of * 2 + one
            cols, inside = head_window(h)
            scores = nt(q_v[:, cols] * inside, k_v[:, cols]) * scale
            top = jnp.max(scores, axis=1, keepdims=True)
            e = jnp.exp(scores - top)
            weights = e * (1.0 / jnp.sum(e, axis=1, keepdims=True))
            attn_v[h] = weights
            acc_v[0, :, cols] += nn(weights.astype(BF16), v_v[:, cols] * inside)

    @pl.loop(0, 5)
    def _(n):
        cols = pl.ds(pl.multiple_of(n * 256, 256), 256)
        mixed_v[:, cols] = acc_v[0, :, cols].astype(BF16)

    loads[4].wait()
    loads[5].wait()

    @pl.loop(0, 5)
    def _(n):
        cols = pl.ds(pl.multiple_of(n * 256, 256), 256)
        stream = res_v[:, cols].astype(F32) + nn(mixed_v[...], proj_v[:, cols])
        acc_v[2, :, cols] = stream.astype(BF16).astype(F32)

    gain_row = gain_ref[...]

    @pl.loop(0, 8)
    def _(b):
        rows = pl.ds(pl.multiple_of(b * 32, 32), 32)
        stream = acc_v[2, rows, :]
        centred = stream - jnp.mean(stream, axis=1, keepdims=True)
        rstd = lax.rsqrt(jnp.mean(centred * centred, axis=1, keepdims=True) + EPS)
        scaled = centred * rstd
        acc_v[2, rows, :] = scaled
        rstd_v[rows, :] = jnp.broadcast_to(rstd, (32, 128))
        enter_v[rows, :] = (scaled * gain_row).astype(BF16)

    @pl.loop(0, 5)
    def _(n):
        rows = nn(pick_v[...], two_lanes(enter_v, n))
        send_b[:, :, pl.ds(pl.multiple_of(n * 128, 128), 128)] = pack(rows)

    own_enter = dispatch(1, send_b, enter_recv)

    pair_mixed = pair(2, mixed_v, mixed_p)
    pair_mixed.start()

    @pl.loop(0, 8)
    def _(b):
        rows = pl.ds(pl.multiple_of(b * 32, 32), 32)
        total = cot_v[0, rows, :].astype(F32)
        for m in range(1, MEMBERS):
            total += cot_v[m, rows, :].astype(F32)
        acc_v[0, rows, :] = total

    def unpack_rows(src, dst, start, count):
        @pl.loop(0, count // 8)
        def _(g):
            chunk = src[pl.ds(start + g * 8, 8)].astype(F32)
            rows = pl.ds(pl.multiple_of(start * 8 + g * 64, 64), 64)
            dst[rows, :HALF] = chunk[:, :CAP, :].reshape(64, HALF).astype(BF16)
            dst[rows, HALF:] = chunk[:, CAP:, :].reshape(64, HALF).astype(BF16)

    own_grad.wait()
    wait_landed(0, grad_recv, 1, 31)
    wait_landed(1, grad_recv, 32, 32)
    unpack_rows(grad_recv, grad_v, 0, CHIPS)
    pair_grad = pair(3, grad_v, grad_p)
    pair_grad.start()
    loads[6].wait()
    pair_second.wait_recv()

    @pl.loop(0, 10)
    def _(t):
        cols = pl.ds(pl.multiple_of(t * 256, 256), 256)
        dpre_v[:, cols] = nt(grad_v[...], second_v[cols, :]).astype(BF16)

    wait_sent(0, send_a, 63)
    loads[7].wait()
    pair_first.wait_recv()

    diagonal = jnp.where(
        lax.broadcasted_iota(jnp.int32, (CAP, 128), 0) == lax.broadcasted_iota(jnp.int32, (CAP, 128), 1), 1.0, 0.0
    )
    pair_enter = []
    for b in range(ROWS // BLOCK):
        chunks = BLOCK // CAP
        if b == 0:
            own_enter.wait()
            wait_landed(2, enter_recv, 1, 31)
        else:
            wait_landed(3, enter_recv, 32, 32)
        unpack_rows(enter_recv, enter_rows, b * chunks, chunks)
        block = pl.ds(b * BLOCK, BLOCK)
        item = pair(4 + b, enter_rows.at[block], enter_p.at[block])
        item.start()
        pair_enter.append(item)
        dot_v[...] = jnp.zeros((BLOCK, 128), F32)

        @pl.loop(0, 10)
        def _(t, block=block):
            cols = pl.ds(pl.multiple_of(t * 256, 256), 256)
            pre = nn(enter_rows[block, :], first_v[:, cols])
            value, slope = gelu_with_grad(pre)
            hidden = value.astype(BF16)
            d_hidden = dpre_v[block, cols].astype(F32)
            hidden_v[block, cols] = hidden
            dpre_v[block, cols] = (slope * d_hidden).astype(BF16)
            both = hidden.astype(F32) * d_hidden
            dot_v[...] += both[:, :128] + both[:, 128:]

        @pl.loop(0, 5)
        def _(n, block=block, b=b, chunks=chunks):
            low = pl.ds(pl.multiple_of(n * 128, 128), 128)
            high = pl.ds(pl.multiple_of(HALF + n * 128, 128), 128)
            weights = jnp.concatenate([first_v[low, :], first_v[high, :]], axis=0)
            send_a[b * chunks : (b + 1) * chunks, :, low] = pack(nt(dpre_v[block, :], weights))

        if b == 0:
            own_back = pltpu.make_async_copy(send_a.at[0], back_recv.at[chip], local_sem.at[2])
            own_back.start()

        @pl.loop(max(1, b * chunks), (b + 1) * chunks)
        def _(n):
            pltpu.make_async_remote_copy(
                send_a.at[n], back_recv.at[chip], a2a_send.at[2], a2a_recv.at[4],
                device_id=(core, behind(n)), device_id_type=MESH,
            ).start()

        dots = jnp.sum(dot_v[...], axis=1, keepdims=True).reshape(chunks, CAP, 1)
        gate_send[b * chunks : (b + 1) * chunks] = jnp.sum(dots * diagonal, axis=1, keepdims=True)

    pair_hidden = pair(6, hidden_v.at[:, pl.ds(D, D)], hidden_p)
    pair_dpre = pair(7, dpre_v.at[:, pl.ds(D, D)], dpre_p)
    pair_hidden.start()
    pair_dpre.start()

    own_gate = pltpu.make_async_copy(gate_send.at[0], gate_recv.at[chip], local_sem.at[3])
    own_gate.start()

    @pl.loop(1, CHIPS)
    def _(n):
        pltpu.make_async_remote_copy(
            gate_send.at[n], gate_recv.at[chip], a2a_send.at[3], a2a_recv.at[5],
            device_id=(core, behind(n)), device_id_type=MESH,
        ).start()

    pair_grad.wait_recv()
    for item in pair_enter:
        item.wait_recv()
    pair_hidden.wait_recv()

    @pl.loop(0, 5)
    def _(t):
        cols = pl.ds(pl.multiple_of(t * 256, 256), 256)
        total = tn(hidden_v[:, cols], grad_v[...]) + tn(hidden_p[:, cols], grad_p[...])
        second_v[cols, :] = total.astype(BF16)

    store_second = pltpu.make_async_copy(second_v.at[pl.ds(0, D)], second_out.at[0], store_sem.at[0])
    store_second.start()
    pair_dpre.wait_recv()

    @pl.loop(0, 5)
    def _(t):
        cols = pl.ds(pl.multiple_of(t * 256, 256), 256)
        total = tn(enter_rows[:, cols], dpre_v[:, :D]) + tn(enter_p[:, cols], dpre_p[...])
        first_v[cols, :D] = total.astype(BF16)

    store_first = pltpu.make_async_copy(first_v.at[:, pl.ds(0, D)], first_out.at[0], store_sem.at[1])
    store_first.start()

    own_back.wait()
    wait_landed(4, back_recv, 0, 63)

    @pl.loop(0, 5)
    def _(n):
        low = pl.ds(pl.multiple_of(n * 128, 128), 128)
        high = pl.ds(pl.multiple_of(HALF + n * 128, 128), 128)
        chunk = back_recv[:, :, low].astype(F32)
        rows = jnp.concatenate(
            [chunk[:, :CAP, :].reshape(ROWS, 128), chunk[:, CAP:, :].reshape(ROWS, 128)], axis=1
        ).astype(BF16)
        total = tn(pick_v[...], rows)
        acc_v[1, :, low] = total[:, :128]
        acc_v[1, :, high] = total[:, 128:]

    @pl.loop(0, 8)
    def _(b):
        rows = pl.ds(pl.multiple_of(b * 32, 32), 32)
        d_norm = acc_v[1, rows, :]
        scaled = acc_v[2, rows, :]
        by_gain = (d_norm * scaled).astype(BF16)
        d_scaled = d_norm * gain_row
        mean_d = jnp.mean(d_scaled, axis=1, keepdims=True)
        mean_ds = jnp.mean(d_scaled * scaled, axis=1, keepdims=True)
        d_stream = rstd_v[rows, :1] * (d_scaled - mean_d - scaled * mean_ds)
        grad = (acc_v[0, rows, :] + d_stream).astype(BF16)
        resid_v[rows, :] = grad
        for half in range(2):
            rg_v[half, rows, :HALF] = grad[:, half * HALF : (half + 1) * HALF]
            rg_v[half, rows, HALF:] = by_gain[:, half * HALF : (half + 1) * HALF]

    pair_rg = pair(8, rg_v.at[1 - core], rg_p)
    pair_rg.start()
    store_resid = pltpu.make_async_copy(resid_v, resid_out, store_sem.at[2])
    store_resid.start()

    @pl.loop(0, 5)
    def _(n):
        cols = pl.ds(pl.multiple_of(n * 256, 256), 256)
        dmix_v[:, cols] = nt(resid_v[...], proj_v[cols, :]).astype(BF16)

    pair_mixed.wait_recv()
    pair_rg.wait_recv()
    loads[8].wait()
    for n, (order, at) in enumerate(((0, 0), (1, 0), (1, HALF))):
        perm_v[n, 0] = nn(rg_v[core, :, at : at + HALF], order_v[order]).astype(BF16)
        perm_v[n, 1] = nn(rg_p[:, at : at + HALF], order_v[order]).astype(BF16)

    @pl.loop(0, 5)
    def _(t):
        cols = pl.ds(pl.multiple_of(t * 128, 128), 128)
        sum1[0, cols, :] = (
            tn(rg_v[core, :, cols], mixed_v[:, :LANES]) + tn(rg_p[:, cols], mixed_p[:, :LANES])
        ).astype(BF16)
        sum1[1, cols, :] = (
            tn(perm_v[0, 0, :, cols], mixed_v[:, LANES : 2 * LANES])
            + tn(perm_v[0, 1, :, cols], mixed_p[:, LANES : 2 * LANES])
        ).astype(BF16)
        sum1[2, cols, :256] = (
            tn(perm_v[1, 0, :, cols], mixed_v[:, 2 * LANES :]) + tn(perm_v[1, 1, :, cols], mixed_p[:, 2 * LANES :])
        ).astype(BF16)
        ones = jnp.ones((TOK, 256), BF16)
        sum1[2, cols, 256:] = (tn(perm_v[2, 0, :, cols], ones) + tn(perm_v[2, 1, :, cols], ones)).astype(BF16)

    axes = ((0, 1, 2), (1, 0, 2), (2, 0, 1))

    def hop(stage, part, o):
        axis = axes[part][stage]
        to = (place[axis] + o) % 4
        spot = [to if a == axis else place[a] for a in range(3)]
        target = spot[0] * 16 + spot[1] * 4 + spot[2]
        if stage == 0:
            src, dst = sum1.at[part, pl.ds(pl.multiple_of(to * 160, 160), 160)], recv1.at[part, o - 1]
        elif stage == 1:
            src, dst = sum2.at[part, to], recv2.at[part, o - 1]
        else:
            src, dst = sum3.at[part, to], recv3.at[part, o - 1]
        n = (stage * 3 + part) * 3 + o - 1
        return pltpu.make_async_remote_copy(
            src, dst, rs_send.at[n], rs_recv.at[n], device_id=(core, target), device_id_type=MESH
        )

    hops = [[hop(s, p, o) for p in range(3) for o in (1, 3, 2)] for s in range(3)]

    def gathered(stage, part):
        mine = place[axes[part][stage]]
        if stage == 0:
            own, others = sum1[part, pl.ds(pl.multiple_of(mine * 160, 160), 160), :], recv1
        elif stage == 1:
            own, others = sum2[part, mine], recv2
        else:
            own, others = sum3[part, mine], recv3
        total = own.astype(F32)
        for o in range(3):
            total += others[part, o].astype(F32)
        return total

    for item in hops[0]:
        item.start()

    acc_v[...] = jnp.zeros((3, TOK, D), F32)

    def attention_back(start, stop):
        @pl.loop(start, stop)
        def _(pair_of):
            for one in range(2):
                h = pair_of * 2 + one
                cols, inside = head_window(h)
                d_mixed = dmix_v[:, cols] * inside
                weights = attn_v[h]
                d_weights = nt(d_mixed, v_v[:, cols])
                shift = jnp.sum(d_weights * weights, axis=1, keepdims=True)
                d_scores = (weights * (d_weights - shift) * scale).astype(BF16)
                acc_v[0, :, cols] += nn(d_scores, k_v[:, cols] * inside)
                acc_v[1, :, cols] += tn(d_scores, q_v[:, cols] * inside)
                acc_v[2, :, cols] += tn(weights.astype(BF16), d_mixed)

    attention_back(0, 5)
    for item in hops[0]:
        item.wait_recv()
    for part in range(3):
        total = gathered(0, part)
        for t in range(4):
            sum2[part, t] = jnp.concatenate([total[t * 40 : (t + 1) * 40], jnp.zeros((8, LANES), F32)], axis=0).astype(BF16)
    for item in hops[1]:
        item.start()

    attention_back(5, 7)
    for item in hops[1]:
        item.wait_recv()
    row = lax.broadcasted_iota(jnp.int32, (16, 48), 0)
    col = lax.broadcasted_iota(jnp.int32, (16, 48), 1)
    for part in range(3):
        total = gathered(1, part).astype(BF16)
        for t in range(4):
            chosen = jnp.where((col == row + SHARE * t) & (row < SHARE), 1.0, 0.0).astype(BF16)
            sum3[part, t] = nn(chosen, total).astype(BF16)
    for item in hops[2]:
        item.start()

    attention_back(7, 8)
    stores = []
    for n, (staged, out) in enumerate(((q_v, q_out), (k_v, k_out), (v_v, v_out))):

        @pl.loop(0, 5)
        def _(t, n=n, staged=staged):
            cols = pl.ds(pl.multiple_of(t * 256, 256), 256)
            staged[:, cols] = acc_v[n, :, cols].astype(BF16)

        item = pltpu.make_async_copy(staged, out, store_sem.at[3 + n])
        item.start()
        stores.append(item)

    own_gate.wait()
    wait_landed(5, gate_recv, 0, 63)
    for m in range(MEMBERS):
        dots = gate_recv[m * 16 : (m + 1) * 16] * diagonal
        dots = jnp.sum(dots, axis=2, keepdims=True).reshape(128, 1)
        total = jnp.sum(pick_v[m * 128 : (m + 1) * 128, :].astype(F32) * dots, axis=0, keepdims=True)
        gate_out[m : m + 1, :] = total / gates_ref[m : m + 1, :]

    for item in hops[2]:
        item.wait_recv()
    for part in range(3):
        share_out[:, part * LANES : (part + 1) * LANES] = gathered(2, part)

    for stage in hops:
        for item in stage:
            item.wait_send()
    wait_sent(1, send_b, 63)
    wait_sent(2, send_a, 63)
    wait_sent(3, gate_send, 63)
    for item in (pair_second, pair_first, pair_mixed, pair_grad, *pair_enter, pair_hidden, pair_dpre, pair_rg):
        item.wait_send()
    for item in (store_second, store_first, store_resid, *stores):
        item.wait()


def shards(queries, keys_in, values_in, resid, out_proj, ln_gain, w_in, w_out, route, slot, gates, cotangent):
    any_spec = pl.BlockSpec(memory_space=pl.ANY)
    vmem_spec = pl.BlockSpec(memory_space=pltpu.VMEM)
    order = jnp.asarray(block_orders(), BF16)
    tokens = jax.ShapeDtypeStruct((TOK, D), BF16)
    square = jax.ShapeDtypeStruct((1, D, D), BF16)
    bf = lambda *shape: pltpu.VMEM(shape, BF16)
    fl = lambda *shape: pltpu.VMEM(shape, F32)
    dma = lambda n: pltpu.SemaphoreType.DMA((n,))
    resid_grad, query_grad, key_grad, value_grad, share, gate_grad, first_grad, second_grad = pl.pallas_call(
        kernel,
        out_shape=(
            tokens, tokens, tokens, tokens,
            jax.ShapeDtypeStruct((16, 3 * LANES), F32),
            jax.ShapeDtypeStruct((MEMBERS, TOK), F32),
            square, square,
        ),
        in_specs=[any_spec] * 5 + [vmem_spec] + [any_spec] * 2 + [vmem_spec] * 3 + [any_spec] * 2,
        out_specs=(any_spec,) * 4 + (vmem_spec,) * 2 + (any_spec,) * 2,
        scratch_shapes=[
            bf(TOK, D), bf(TOK, D), bf(TOK, D), bf(TOK, D), bf(D, D), bf(MEMBERS, TOK, D), bf(2, HALF, HALF),
            bf(D, H), bf(H, D),
            fl(HEADS, TOK, TOK), fl(3, TOK, D), bf(TOK, D), bf(TOK, D), fl(TOK, 128), bf(TOK, D), bf(ROWS, TOK),
            bf(CHIPS, 16, HALF), bf(CHIPS, 16, HALF), bf(CHIPS, 16, HALF), bf(CHIPS, 16, HALF), bf(CHIPS, 16, HALF),
            bf(ROWS, D), bf(ROWS, D), bf(ROWS, D), bf(ROWS, D), bf(ROWS, H), bf(ROWS, H), bf(ROWS, D), bf(ROWS, D),
            fl(BLOCK, 128),
            bf(2, TOK, D), bf(TOK, D), bf(3, 2, TOK, HALF), bf(TOK, D), bf(TOK, D),
            fl(CHIPS, 1, 128), fl(CHIPS, 1, 128),
            bf(3, HALF, LANES), bf(3, 3, 160, LANES), bf(3, 4, 48, LANES), bf(3, 3, 48, LANES),
            bf(3, 4, 16, LANES), bf(3, 3, 16, LANES),
            dma(9), dma(6), dma(4), dma(9), dma(9), dma(4), dma(6), dma(27), dma(27),
        ],
        compiler_params=pltpu.CompilerParams(
            collective_id=0, has_side_effects=True, vmem_limit_bytes=63 * 1024 * 1024
        ),
        cost_estimate=pl.CostEstimate(flops=25_000_000_000, bytes_accessed=40_000_000, transcendentals=4_000_000),
    )(queries, keys_in, values_in, resid, out_proj, ln_gain[None], w_in, w_out, route, slot, gates, cotangent, order)
    proj_grad = share[:SHARE, :D].T
    gain_grad = share[:SHARE, D]
    return (
        resid_grad, query_grad, key_grad, value_grad, proj_grad, gain_grad, gate_grad, first_grad, second_grad,
    )


def solution(mesh):
    both = ("dp", "expert")
    return jax.shard_map(
        shards,
        mesh=mesh,
        in_specs=(
            P(both, None), P(both, None), P(both, None), P(both, None), P(), P(),
            P("expert", None, "dp"), P("expert", "dp", None),
            P(None, both), P(None, both), P(None, both), P(None, both, None),
        ),
        out_specs=(
            P(both, None), P(both, None), P(both, None), P(both, None), P(None, both), P(both), P(None, both),
            P("expert", None, "dp"), P("expert", "dp", None),
        ),
        check_vma=False,
    )
```

time: 261 us -> 125 us (0.48)
  Pallas kernels: 0 us -> 107 us
  matrix products: 73 us -> 0 us
  blocking collectives: 57.7 us -> 0 us
  waiting for transfers between devices: 53.9 us -> 0 us
  other arithmetic: 19.8 us -> 0 us
  starting transfers between devices: 16.7 us -> 0 us
  between operations: 14.1 us -> 0.68 us
  local copies, waits for them, and re-layouts: 24.7 us -> 16.4 us
    pallas_call x0 -> x1, Pallas kernels: none -> 107 us  [shards(): pl.pallas_call(kernel, out_shape=(tokens, tokens, tokens, tokens, jax.Sha...]
    dot_general x16 -> x0, matrix products: 68.1 us -> none  [the longest x1 17.2 us: shards(): jnp.dot(grad_rows, w_second.T, preferred_element_type=jnp.float32)]
    all_to_all x2 -> x0, blocking collectives: 57.7 us -> none  [to_expert(): lax.all_to_all(buffer, 'expert', split_axis=0, concat_axis=0, tiled=True)]
    all_to_all x2 -> x0, waiting for transfers between devices: 38.1 us -> none  [the longest x1 19.6 us: to_tokens(): lax.all_to_all(mine, 'expert', split_axis=0, concat_axis=0, tiled=True)]
    all_to_all x2 -> x0, starting transfers between devices: 16.1 us -> none  [the longest x1 10.6 us: to_tokens(): lax.all_to_all(mine, 'expert', split_axis=0, concat_axis=0, tiled=True)]
    reduce_scatter x2 -> x0, waiting for transfers between devices: 14.6 us -> none  [the longest x1 14.6 us: to_tokens(): lax.psum_scatter(partial_sums.astype(jnp.bfloat16), 'dp', scatter_dimensi...]
    reduce_sum x6 -> x0, other arithmetic: 11.4 us -> none  [the longest x1 4.75 us: shards(): jnp.sum(hidden.astype(jnp.float32) * d_hidden, axis=-1, keepdims=True)]
    sub x1 -> x0, matrix products: 4.88 us -> none  [attend(): jax.nn.softmax(scores, axis=-1).astype(jnp.bfloat16).astype(jnp.float32)]
  transfers between devices with their start and end apart: 6 -> 0, of which waited for: 4 -> 0; matrix products, arithmetic and copies ran while one was open for 21% -> 0% of each run, Pallas kernels for 0% -> 0%
where the time goes in v2:
time: 125 us
  Pallas kernels  107 us (86%)
  local copies, waits for them, and re-layouts  16.4 us (13%)
    pallas_call x1, Pallas kernels, shards(): pl.pallas_call(kernel, out_shape=(tokens, tokens, tokens, tokens, jax.Sha...  107 us
    unnamed x15, local copies, waits for them, and re-layouts  12.2 us

profile of v2, /device:TPU:0, one launch (start us, length us, event | category | flops | bytes accessed | tf_op | source)
XLA Modules:
  0.0 124.6 jit_solution(8655154705081487632)
XLA Ops:
  0.6 1.3 %broadcast_in_dim.3.gain_ref = f32[1,1280]{1,0:T(1,128)} reshape(f32[1280]{0:T(1024)} %param.18) | data formatting | bytes 10240 | tf_op jit(solution)/shard_map/broadcast_in_dim | solution.py:584
  1.9 107.5 %shard_map.196 = (bf16[256,1280]{1,0:T(8,128)(2,1)}, bf16[256,1280]{1,0:T(8,128)(2,1)}, bf16[256,1280]{1,0:T(8,128)(2,1)}, bf16[256,1280]{1,0:T(8,128)(2,1)}, f3...) custom-call(bf16[256,1280]{1,0:T(8,128)(2,1)} %q_in.1, ...), custom_call_target="tpu_custom_call" | custom-call | flops 24999999488 | bytes 40000000 | tf_op jit(solution)/shard_map/pallas_call | solution.py:557
  109.4 0.0 copy-start.2
  109.4 0.0 copy-start.3
  109.4 0.0 copy-start.1
  109.4 1.5 %slice_reduce_fusion = f32[10]{0:T(128)} fusion(f32[16,1536]{1,0:T(8,128)} %get-tuple-element.21), kind=kLoop, calls=%fused_computation.1 | loop fusion | bytes 80 | tf_op jit(solution)/shard_map/slice | solution.py:586
  110.9 1.5 %slice_bitcast_fusion = f32[1280,10]{0,1:T(8,128)} fusion(f32[16,1536]{1,0:T(8,128)} %get-tuple-element.21), kind=kLoop, calls=%fused_computation | loop fusion | bytes 102400 | tf_op jit(solution)/shard_map/transpose | solution.py:585
  112.4 2.0 %copy.29 = bf16[256,1280]{1,0:T(8,128)(2,1)} copy(bf16[256,1280]{1,0:T(8,128)(2,1)} %get-tuple-element.34) | data formatting | bytes 1310720
  114.4 2.0 %copy.30 = bf16[256,1280]{1,0:T(8,128)(2,1)} copy(bf16[256,1280]{1,0:T(8,128)(2,1)} %get-tuple-element.35) | data formatting | bytes 1310720
  116.4 2.0 %copy.31 = bf16[256,1280]{1,0:T(8,128)(2,1)} copy(bf16[256,1280]{1,0:T(8,128)(2,1)} %get-tuple-element.36) | data formatting | bytes 1310720
  118.3 0.0 copy-done.2
  118.3 0.8 copy.32
  119.2 0.0 copy-done.3
  119.2 0.6 copy.33
  119.8 0.0 copy-done.1
  119.8 0.0 copy-start
  119.8 1.7 %copy.34 = bf16[1,1280,1280]{2,1,0:T(8,128)(2,1)} copy(bf16[1,1280,1280]{2,1,0:T(8,128)(2,1)S(1)} %copy-done.1) | data formatting | bytes 6553600
  121.5 1.4 %copy-done = bf16[1,1280,1280]{2,1,0:T(8,128)(2,1)S(1)} copy-done((bf16[1,1280,1280]{2,1,0:T(8,128)(2,1)S(1)}, bf16[1,1280,1280]{2,1,0:T(8,128)(2,1)}, u32[]{:S(2)}) %copy-start) | copy-done | bytes 3276824
  122.9 1.7 %copy.35 = bf16[1,1280,1280]{2,1,0:T(8,128)(2,1)} copy(bf16[1,1280,1280]{2,1,0:T(8,128)(2,1)S(1)} %copy-done) | data formatting | bytes 6553600
Async XLA Ops:
  109.4 8.9 %copy-start.2 = (bf16[256,1280]{1,0:T(8,128)(2,1)S(1)}, bf16[256,1280]{1,0:T(8,128)(2,1)}, u32[]{:S(2)}) copy-start(bf16[256,1280]{1,0:T(8,128)(2,1)} %get-tuple-element.37) | copy-start | bytes 1966084
  109.4 9.8 %copy-start.3 = (f32[4,256]{1,0:T(4,128)S(1)}, f32[4,256]{1,0:T(4,128)}, u32[]{:S(2)}) copy-start(f32[4,256]{1,0:T(4,128)} %get-tuple-element.40) | copy-start | bytes 12292
  109.4 10.3 %copy-start.1 = (bf16[1,1280,1280]{2,1,0:T(8,128)(2,1)S(1)}, bf16[1,1280,1280]{2,1,0:T(8,128)(2,1)}, u32[]{:S(2)}) copy-start(bf16[1,1280,1280]{2,1,0:T(8,128)(2,1)} %get-tuple-element.41) | copy-start | bytes 9830404
  119.8 3.1 %copy-start = (bf16[1,1280,1280]{2,1,0:T(8,128)(2,1)S(1)}, bf16[1,1280,1280]{2,1,0:T(8,128)(2,1)}, u32[]{:S(2)}) copy-start(bf16[1,1280,1280]{2,1,0:T(8,128)(2,1)} %get-tuple-element.42) | copy-start | bytes 9830404

commit v3 on v2

--- a/solution.py
+++ b/solution.py
@@ -58,10 +58,12 @@
 
 
 def gelu_with_grad(x):
-    u = 1.0 / (1.0 + (0.3275911 * math.sqrt(0.5)) * jnp.abs(x))
-    poly = u * (0.254829592 + u * (-0.284496736 + u * (1.421413741 + u * (-1.453152027 + u * 1.061405429))))
-    e = jnp.exp(-0.5 * x * x)
-    tail = 0.5 * poly * e
+    below = 1.0 + (0.3275911 * math.sqrt(0.5)) * jnp.abs(x)
+    u = pl.reciprocal(below, approx=True)
+    u = u * (2.0 - below * u)
+    e = jnp.exp(x * x * -0.5)
+    poly = u * (0.127414796 + u * (-0.142248368 + u * (0.7107068705 + u * (-0.7265760135 + u * 0.5307027145))))
+    tail = poly * e
     cdf = jnp.where(x >= 0.0, 1.0 - tail, tail)
     return x * cdf, cdf + x * (e * (1.0 / math.sqrt(2.0 * math.pi)))
 
@@ -90,17 +92,15 @@
     chip = lax.axis_index("expert")
     place = (chip // 16, (chip // 4) % 4, chip % 4)
 
-    def offsets(n):
-        q = n // 16
-        return ((q % 2) * 2 + q // 2, (n // 4) % 4, n % 4)
+    around = [[p] + [lax.rem(p + o, 4) for o in range(1, 4)] for p in place]
 
     def ahead(n):
-        o = offsets(n)
-        return ((place[0] + o[0]) % 4) * 16 + ((place[1] + o[1]) % 4) * 4 + (place[2] + o[2]) % 4
+        o = ((0, 2, 1, 3)[n // 16], (n // 4) % 4, n % 4)
+        return around[0][o[0]] * 16 + around[1][o[1]] * 4 + around[2][o[2]]
 
     def behind(n):
-        o = offsets(n)
-        return ((place[0] + 4 - o[0]) % 4) * 16 + ((place[1] + 4 - o[1]) % 4) * 4 + (place[2] + 4 - o[2]) % 4
+        o = ((0, 2, 3, 1)[n // 16], -(n // 4) % 4, -n % 4)
+        return around[0][o[0]] * 16 + around[1][o[1]] * 4 + around[2][o[2]]
 
     def load(n, src, dst):
         return pltpu.make_async_copy(src, dst, load_sem.at[n])
@@ -121,8 +121,7 @@
 
     barrier = pltpu.get_barrier_semaphore()
 
-    @pl.loop(1, CHIPS)
-    def _(n):
+    for n in range(1, CHIPS):
         pl.semaphore_signal(barrier, inc=1, device_id=(core, ahead(n)), device_id_type=MESH)
 
     pl.semaphore_signal(barrier, inc=1, device_id=(1 - core, chip), device_id_type=MESH)
@@ -156,8 +155,7 @@
         own = pltpu.make_async_copy(src.at[chip], dst.at[0], local_sem.at[which])
         own.start()
 
-        @pl.loop(1, CHIPS)
-        def _(n):
+        for n in range(1, CHIPS):
             to = ahead(n)
             pltpu.make_async_remote_copy(
                 src.at[to], dst.at[n], a2a_send.at[which], a2a_recv.at[which * 2 + n // 32],
@@ -194,10 +192,10 @@
     loads[3].wait()
     scale = 1.0 / math.sqrt(HEAD)
 
-    @pl.loop(0, HEADS // 2)
-    def _(pair_of):
-        for one in range(2):
-            h = pair_of * 2 + one
+    @pl.loop(0, HEADS // 4)
+    def _(four):
+        for one in range(4):
+            h = four * 4 + one
             cols, inside = head_window(h)
             scores = nt(q_v[:, cols] * inside, k_v[:, cols]) * scale
             top = jnp.max(scores, axis=1, keepdims=True)
@@ -220,7 +218,7 @@
         stream = res_v[:, cols].astype(F32) + nn(mixed_v[...], proj_v[:, cols])
         acc_v[2, :, cols] = stream.astype(BF16).astype(F32)
 
-    gain_row = gain_ref[...]
+    gain_row = gain_ref[...].reshape(1, D)
 
     @pl.loop(0, 8)
     def _(b):
@@ -295,7 +293,9 @@
         pair_enter.append(item)
         dot_v[...] = jnp.zeros((BLOCK, 128), F32)
 
-        @pl.loop(0, 10)
+        dot_v[...] = jnp.zeros((BLOCK, 128), F32)
+
+        @pl.loop(0, 10, unroll=2)
         def _(t, block=block):
             cols = pl.ds(pl.multiple_of(t * 256, 256), 256)
             pre = nn(enter_rows[block, :], first_v[:, cols])
@@ -304,7 +304,7 @@
             d_hidden = dpre_v[block, cols].astype(F32)
             hidden_v[block, cols] = hidden
             dpre_v[block, cols] = (slope * d_hidden).astype(BF16)
-            both = hidden.astype(F32) * d_hidden
+            both = value * d_hidden
             dot_v[...] += both[:, :128] + both[:, 128:]
 
         @pl.loop(0, 5)
@@ -318,8 +318,7 @@
             own_back = pltpu.make_async_copy(send_a.at[0], back_recv.at[chip], local_sem.at[2])
             own_back.start()
 
-        @pl.loop(max(1, b * chunks), (b + 1) * chunks)
-        def _(n):
+        for n in range(max(1, b * chunks), (b + 1) * chunks):
             pltpu.make_async_remote_copy(
                 send_a.at[n], back_recv.at[chip], a2a_send.at[2], a2a_recv.at[4],
                 device_id=(core, behind(n)), device_id_type=MESH,
@@ -336,8 +335,7 @@
     own_gate = pltpu.make_async_copy(gate_send.at[0], gate_recv.at[chip], local_sem.at[3])
     own_gate.start()
 
-    @pl.loop(1, CHIPS)
-    def _(n):
+    for n in range(1, CHIPS):
         pltpu.make_async_remote_copy(
             gate_send.at[n], gate_recv.at[chip], a2a_send.at[3], a2a_recv.at[5],
             device_id=(core, behind(n)), device_id_type=MESH,
@@ -471,9 +469,9 @@
 
     def attention_back(start, stop):
         @pl.loop(start, stop)
-        def _(pair_of):
-            for one in range(2):
-                h = pair_of * 2 + one
+        def _(four):
+            for one in range(4):
+                h = four * 4 + one
                 cols, inside = head_window(h)
                 d_mixed = dmix_v[:, cols] * inside
                 weights = attn_v[h]
@@ -484,7 +482,7 @@
                 acc_v[1, :, cols] += tn(d_scores, q_v[:, cols] * inside)
                 acc_v[2, :, cols] += tn(weights.astype(BF16), d_mixed)
 
-    attention_back(0, 5)
+    attention_back(0, 2)
     for item in hops[0]:
         item.wait_recv()
     for part in range(3):
@@ -494,7 +492,7 @@
     for item in hops[1]:
         item.start()
 
-    attention_back(5, 7)
+    attention_back(2, 3)
     for item in hops[1]:
         item.wait_recv()
     row = lax.broadcasted_iota(jnp.int32, (16, 48), 0)
@@ -507,7 +505,7 @@
     for item in hops[2]:
         item.start()
 
-    attention_back(7, 8)
+    attention_back(3, 4)
     stores = []
     for n, (staged, out) in enumerate(((q_v, q_out), (k_v, k_out), (v_v, v_out))):
 
@@ -542,6 +540,38 @@
     for item in (pair_second, pair_first, pair_mixed, pair_grad, *pair_enter, pair_hidden, pair_dpre, pair_rg):
         item.wait_send()
     for item in (store_second, store_first, store_resid, *stores):
+        item.wait()
+
+
+def finish(
+    resid_in, q_in, k_in, v_in, first_in, second_in, share_ref, gate_ref,
+    resid_out, q_out, k_out, v_out, first_out, second_out, proj_out, gain_out, gate_out,
+    wide_v, rows_v, sem,
+):
+    pieces = [
+        (first_in.at[0, pl.ds(0, HALF)], first_out.at[0, pl.ds(0, HALF)], wide_v.at[0, 0]),
+        (second_in.at[0, pl.ds(0, HALF)], second_out.at[0, pl.ds(0, HALF)], wide_v.at[1, 0]),
+        (first_in.at[0, pl.ds(HALF, HALF)], first_out.at[0, pl.ds(HALF, HALF)], wide_v.at[0, 1]),
+        (second_in.at[0, pl.ds(HALF, HALF)], second_out.at[0, pl.ds(HALF, HALF)], wide_v.at[1, 1]),
+        (resid_in, resid_out, rows_v.at[0]),
+        (q_in, q_out, rows_v.at[1]),
+        (k_in, k_out, rows_v.at[2]),
+        (v_in, v_out, rows_v.at[3]),
+    ]
+    loads = [pltpu.make_async_copy(src, held, sem.at[0, n]) for n, (src, _, held) in enumerate(pieces)]
+    stores = [pltpu.make_async_copy(held, dst, sem.at[1, n]) for n, (_, dst, held) in enumerate(pieces)]
+    for item in loads:
+        item.start()
+    for load, store in zip(loads, stores):
+        load.wait()
+        store.start()
+    proj_out[...] = share_ref[:SHARE, :D]
+    row = lax.broadcasted_iota(jnp.int32, (16, 128), 0)
+    col = lax.broadcasted_iota(jnp.int32, (16, 128), 1)
+    gain = jnp.sum(jnp.where(row == col, share_ref[:, D : D + 128], 0.0), axis=0, keepdims=True)
+    gain_out[...] = gain[:, :SHARE]
+    gate_out[...] = gate_ref[...]
+    for item in stores:
         item.wait()
 
 
@@ -581,11 +611,23 @@
             collective_id=0, has_side_effects=True, vmem_limit_bytes=63 * 1024 * 1024
         ),
         cost_estimate=pl.CostEstimate(flops=25_000_000_000, bytes_accessed=40_000_000, transcendentals=4_000_000),
-    )(queries, keys_in, values_in, resid, out_proj, ln_gain[None], w_in, w_out, route, slot, gates, cotangent, order)
-    proj_grad = share[:SHARE, :D].T
-    gain_grad = share[:SHARE, D]
+    )(queries, keys_in, values_in, resid, out_proj, ln_gain, w_in, w_out, route, slot, gates, cotangent, order)
+    resid_grad, query_grad, key_grad, value_grad, first_grad, second_grad, proj_grad, gain_grad, gate_grad = pl.pallas_call(
+        finish,
+        out_shape=(
+            tokens, tokens, tokens, tokens, square, square,
+            jax.ShapeDtypeStruct((SHARE, D), F32),
+            jax.ShapeDtypeStruct((1, SHARE), F32),
+            jax.ShapeDtypeStruct((MEMBERS, TOK), F32),
+        ),
+        in_specs=[any_spec] * 6 + [vmem_spec] * 2,
+        out_specs=(any_spec,) * 6 + (vmem_spec,) * 3,
+        scratch_shapes=[bf(2, 2, HALF, D), bf(4, TOK, D), pltpu.SemaphoreType.DMA((2, 8))],
+        compiler_params=pltpu.CompilerParams(vmem_limit_bytes=60 * 1024 * 1024),
+    )(resid_grad, query_grad, key_grad, value_grad, first_grad, second_grad, share, gate_grad)
     return (
-        resid_grad, query_grad, key_grad, value_grad, proj_grad, gain_grad, gate_grad, first_grad, second_grad,
+        resid_grad, query_grad, key_grad, value_grad, proj_grad.T, gain_grad.reshape(SHARE), gate_grad,
+        first_grad, second_grad,
     )
 
 

time: 125 us -> 113 us (0.904)
  local copies, waits for them, and re-layouts: 16.4 us -> 0 us
  Pallas kernels: 107 us -> 112 us
    unnamed x15 -> x0, local copies, waits for them, and re-layouts: 12.2 us -> none
    pallas_call x0 -> x1, Pallas kernels: none -> 8.59 us  [shards(): pl.pallas_call(finish, out_shape=(tokens, tokens, tokens, tokens, square,...]
    pallas_call x1, Pallas kernels: 107 us -> 104 us  [shards(): pl.pallas_call(kernel, out_shape=(tokens, tokens, tokens, tokens, jax.Sha...]
    transpose x1 -> x0, local copies, waits for them, and re-layouts: 1.53 us -> none  [shards(): proj_grad = share[:SHARE, :D].T]
    slice x1 -> x0, local copies, waits for them, and re-layouts: 1.47 us -> none  [shards(): gain_grad = share[:SHARE, D]]
    broadcast_in_dim x1 -> x0, local copies, waits for them, and re-layouts: 1.29 us -> none  [shards(): ln_gain[None]]
where the time goes in v3:
time: 113 us
  Pallas kernels  112 us (99%)
    pallas_call x1, Pallas kernels, shards(): pl.pallas_call(kernel, out_shape=(tokens, tokens, tokens, tokens, jax.Sha...  104 us
    pallas_call x1, Pallas kernels, shards(): pl.pallas_call(finish, out_shape=(tokens, tokens, tokens, tokens, square,...  8.59 us

profile of v3, /device:TPU:0, one launch (start us, length us, event | category | flops | bytes accessed | tf_op | source)
XLA Modules:
  0.0 113.0 jit_solution(11074650585685783237)
XLA Ops:
  0.6 103.6 %shard_map.196 = (bf16[256,1280]{1,0:T(8,128)(2,1)}, bf16[256,1280]{1,0:T(8,128)(2,1)}, bf16[256,1280]{1,0:T(8,128)(2,1)}, bf16[256,1280]{1,0:T(8,128)(2,1)}, f3...) custom-call(bf16[256,1280]{1,0:T(8,128)(2,1)} %q_in.1, ...), custom_call_target="tpu_custom_call" | custom-call | flops 24999999488 | bytes 40000000 | tf_op jit(solution)/shard_map/pallas_call | solution.py:587
  104.2 8.6 %shard_map.197 = (bf16[256,1280]{1,0:T(8,128)(2,1)}, bf16[256,1280]{1,0:T(8,128)(2,1)}, bf16[256,1280]{1,0:T(8,128)(2,1)}, bf16[256,1280]{1,0:T(8,128)(2,1)}, bf...) custom-call(bf16[256,1280]{1,0:T(8,128)(2,1)} %get-tuple-element.26., ...), custom_call_target="tpu_custom_call" | custom-call | tf_op jit(solution)/shard_map/pallas_call | solution.py:615

commit v4 on v3

--- a/solution.py
+++ b/solution.py
@@ -354,17 +354,6 @@
 
     store_second = pltpu.make_async_copy(second_v.at[pl.ds(0, D)], second_out.at[0], store_sem.at[0])
     store_second.start()
-    pair_dpre.wait_recv()
-
-    @pl.loop(0, 5)
-    def _(t):
-        cols = pl.ds(pl.multiple_of(t * 256, 256), 256)
-        total = tn(enter_rows[:, cols], dpre_v[:, :D]) + tn(enter_p[:, cols], dpre_p[...])
-        first_v[cols, :D] = total.astype(BF16)
-
-    store_first = pltpu.make_async_copy(first_v.at[:, pl.ds(0, D)], first_out.at[0], store_sem.at[1])
-    store_first.start()
-
     own_back.wait()
     wait_landed(4, back_recv, 0, 63)
 
@@ -464,6 +453,17 @@
 
     for item in hops[0]:
         item.start()
+
+    pair_dpre.wait_recv()
+
+    @pl.loop(0, 5)
+    def _(t):
+        cols = pl.ds(pl.multiple_of(t * 256, 256), 256)
+        total = tn(enter_rows[:, cols], dpre_v[:, :D]) + tn(enter_p[:, cols], dpre_p[...])
+        first_v[cols, :D] = total.astype(BF16)
+
+    store_first = pltpu.make_async_copy(first_v.at[:, pl.ds(0, D)], first_out.at[0], store_sem.at[1])
+    store_first.start()
 
     acc_v[...] = jnp.zeros((3, TOK, D), F32)
 

time: 113 us -> 109 us (0.965)
  Pallas kernels: 112 us -> 108 us
    pallas_call x1, Pallas kernels: 104 us -> 99.5 us  [shards(): pl.pallas_call(kernel, out_shape=(tokens, tokens, tokens, tokens, jax.Sha...]
where the time goes in v4:
time: 109 us
  Pallas kernels  108 us (99%)
    pallas_call x1, Pallas kernels, shards(): pl.pallas_call(kernel, out_shape=(tokens, tokens, tokens, tokens, jax.Sha...  99.5 us
    pallas_call x1, Pallas kernels, shards(): pl.pallas_call(finish, out_shape=(tokens, tokens, tokens, tokens, square,...  8.59 us

profile of v4, /device:TPU:0, one launch (start us, length us, event | category | flops | bytes accessed | tf_op | source)
XLA Modules:
  0.0 108.9 jit_solution(17976578602951702637)
XLA Ops:
  0.6 99.5 %shard_map.196 = (bf16[256,1280]{1,0:T(8,128)(2,1)}, bf16[256,1280]{1,0:T(8,128)(2,1)}, bf16[256,1280]{1,0:T(8,128)(2,1)}, bf16[256,1280]{1,0:T(8,128)(2,1)}, f3...) custom-call(bf16[256,1280]{1,0:T(8,128)(2,1)} %q_in.1, ...), custom_call_target="tpu_custom_call" | custom-call | flops 24999999488 | bytes 40000000 | tf_op jit(solution)/shard_map/pallas_call | solution.py:587
  100.1 8.6 %shard_map.197 = (bf16[256,1280]{1,0:T(8,128)(2,1)}, bf16[256,1280]{1,0:T(8,128)(2,1)}, bf16[256,1280]{1,0:T(8,128)(2,1)}, bf16[256,1280]{1,0:T(8,128)(2,1)}, bf...) custom-call(bf16[256,1280]{1,0:T(8,128)(2,1)} %get-tuple-element.26., ...), custom_call_target="tpu_custom_call" | custom-call | tf_op jit(solution)/shard_map/pallas_call | solution.py:615
